TPU v7x, 32 devices: a whole 2x2x4 slice. The times are simulated.
32 devices in a mesh: group: 2 (over y), replica: 8 (over z, x), tensor: 2 (over core).
Axes of the slice: x: 2, y: 2, z: 4, core: 2. Of those that a mesh axis runs over, the one named last changes fastest.
Arguments:
- queries: bfloat16 [4096, 4096], P(('group', 'replica'), 'tensor'), parts along dimension 0, may hold values from -12 to 12
- keys: bfloat16 [4096, 512], P(('group', 'replica'), 'tensor'), parts along dimension 0, may hold values from -6 to 6
- values: bfloat16 [4096, 512], P(('group', 'replica'), 'tensor'), parts along dimension 0, may hold values from -6 to 6
- lengths: int32 [16], P('group'), parts along dimension 0, may hold values from 1 to 8, as said below
- slot_prompt: int32 [16, 2], P('group'), parts along dimension 0, may hold values from 0 to 7, as said below
- slot_span: int32 [16, 2], P('group'), parts along dimension 0, may hold values from 0 to 7
Outputs:
- attention: bfloat16 [16384, 4096], P(('group', 'replica'), 'tensor'), parts along dimension 0
- cache_keys: bfloat16 [16384, 512], P(('group', 'replica'), 'tensor'), parts along dimension 0
- cache_values: bfloat16 [16384, 512], P(('group', 'replica'), 'tensor'), parts along dimension 0
There are 2 independent parts, one for each index of `group`. A program takes and returns all parts, laid end to end along the dimension named above; each array names one. Nothing has to cross between parts.
Inputs may be any that keep to these rules, and one draw needn't show every extreme that they name: The lengths sum to 16, and some prompt has exactly 8 spans. Every slot holds one span: each pair of a prompt p and a span m < lengths[p] is named by exactly one slot through slot_prompt and slot_span, and no other pair is named. Span m < min(lengths[p], 2) of prompt p sits in slot m of replica p.
All inputs are finite; a program needn't handle non-finite values.
Results may differ from a plain program's by a relative error of at most 0.0047.
Values may be sent and summed in bfloat16 or wider, within the bound.
No kernel may reach another device: no remote copies, remote signals or barrier semaphores. Data moves between devices by JAX's collectives and lax.ppermute only.
A program may use at most 128 MiB of HBM per device.

v0:
```python
import functools
import math

import jax
import jax.numpy as jnp
from jax import lax
from jax.experimental import pallas as pl
from jax.experimental.pallas import tpu as pltpu
from jax.sharding import PartitionSpec as P

HDIM = 128
SPAN = 128
SLOTS = 2
LANES = 128
MAXC = 8
BLOCK = 4
PART = 2
LOG2E = 1.0 / math.log(2.0)
VMEM_BYTES = 40 * 1024 * 1024
MOST_VMEM_BYTES = 60 * 1024 * 1024
LEAST_SUM, MOST_SUM = 1e-20, 1e30
ANY = pl.BlockSpec(memory_space=pl.ANY)
SMEM = pl.BlockSpec(memory_space=pltpu.SMEM)
VMEM = pl.BlockSpec(memory_space=pltpu.VMEM)


def cost_of(us):
    return pl.CostEstimate(flops=int(us * 1.15e9), bytes_accessed=0, transcendentals=0)


def column_ring(replicas):
    return list(range(0, replicas, 2)) + list(range(replicas - 1, 0, -2))


def copy_all(copies):
    for copy in copies:
        copy.start()
    for copy in copies:
        copy.wait()


def pack_kv_kernel(k_ref, v_ref, o_ref, sems):
    copy_all(
        [
            pltpu.make_async_copy(k_ref.at[SPAN:], o_ref.at[:SPAN], sems.at[0]),
            pltpu.make_async_copy(v_ref.at[SPAN:], o_ref.at[SPAN:], sems.at[1]),
        ]
    )


def pack_kv(keys, values):
    return pl.pallas_call(
        pack_kv_kernel,
        out_shape=jax.ShapeDtypeStruct((2 * SPAN, keys.shape[1]), keys.dtype),
        in_specs=[ANY] * 2,
        out_specs=VMEM,
        scratch_shapes=[pltpu.SemaphoreType.DMA((2,))],
        compiler_params=pltpu.CompilerParams(vmem_limit_bytes=MOST_VMEM_BYTES),
        cost_estimate=cost_of(1),
    )(keys, values)


def pack_q_kernel(q_ref, o_top, o_bottom, sems):
    half = SPAN // 2
    copy_all(
        [
            pltpu.make_async_copy(q_ref.at[SPAN : SPAN + half], o_top, sems.at[0]),
            pltpu.make_async_copy(q_ref.at[SPAN + half :], o_bottom, sems.at[1]),
        ]
    )


def pack_q(queries):
    half = jax.ShapeDtypeStruct((SPAN // 2, queries.shape[1]), queries.dtype)
    return pl.pallas_call(
        pack_q_kernel,
        out_shape=(half, half),
        in_specs=[ANY],
        out_specs=(VMEM, VMEM),
        scratch_shapes=[pltpu.SemaphoreType.DMA((2,))],
        compiler_params=pltpu.CompilerParams(vmem_limit_bytes=VMEM_BYTES),
        cost_estimate=cost_of(1),
    )(queries)


def places(lengths, slot_prompt, slot_span):
    replicas = lengths.shape[0]
    mine = lax.axis_index("replica")
    ring = jnp.arange(replicas, dtype=jnp.int32)
    place = jnp.where(mine % 2 == 0, mine // 2, replicas - 1 - mine // 2)
    at = (place + replicas - ring) % replicas
    other = jnp.where(at < replicas // 2, 2 * at, 2 * (replicas - at) - 1)
    chosen = other[:, None] == ring[None, :]
    wanted = chosen & (slot_prompt[None, :, 1] == mine) & (ring[:, None] > 0)
    spans = jnp.where(wanted, slot_span[None, :, 1] + 1, 0)
    whole = jnp.where(chosen & (ring[:, None] == 0), lengths[None, :] + 1, 0)
    table = jnp.sum(spans + whole, axis=1, keepdims=True) - 1
    return jnp.broadcast_to(table, (replicas, LANES))


def entry(meta_ref, n):
    return jnp.max(meta_ref[n : n + 1, :])


def entries(meta_ref, offsets):
    found = {offset: entry(meta_ref, offset) for offset in dict.fromkeys(offsets)}
    return [found[offset] for offset in offsets]


def widen(v_ref, wide_ref):
    for at in range(0, v_ref.shape[-1], HDIM):
        wide_ref[:, 2 * at : 2 * at + HDIM] = v_ref[:, at : at + HDIM]
        wide_ref[:, 2 * at + HDIM : 2 * at + 2 * HDIM] = jnp.ones(
            (v_ref.shape[0], HDIM), v_ref.dtype
        )


def stack(q_ref, stacked):
    kv_heads, rows, _ = stacked.shape
    tall = q_ref.shape[0]
    group = rows // tall
    for shared in range(kv_heads):
        for h in range(group):
            at = (shared * group + h) * HDIM
            stacked[shared, h * tall : (h + 1) * tall, :] = q_ref[:, at : at + HDIM]


def divide(mixed, shared, o_ref, bounds):
    tall = o_ref.shape[0]
    group = mixed.shape[0] // tall
    total = mixed[:, HDIM:]
    inverse = pl.reciprocal(total, approx=True)
    inverse = inverse * (2.0 - total * inverse)
    result = (mixed[:, :HDIM] * inverse).astype(o_ref.dtype)
    for h in range(group):
        at = (shared * group + h) * HDIM
        o_ref[:, at : at + HDIM] = result[h * tall : (h + 1) * tall, :]
    total = total.reshape(-1, 8, HDIM)
    bounds[0] = jnp.minimum(bounds[0], jnp.min(total, axis=0))
    bounds[1] = jnp.maximum(bounds[1], jnp.max(total, axis=0))


def attend_piece(span, start, stacked, k_ref, wide_ref, mixed, o_ref, bounds):
    kv_heads, rows, _ = stacked.shape
    heads = range(kv_heads)
    tall = o_ref.shape[0]
    scale = LOG2E / math.sqrt(HDIM)
    blocks = span // BLOCK
    edge = span % PART * SPAN + start

    def keys_of(block, spans):
        return pl.ds(pl.multiple_of(block * BLOCK * SPAN, BLOCK * SPAN), spans * SPAN)

    def scores(shared, block, spans, masked):
        found = lax.dot_general(
            stacked[shared],
            k_ref[keys_of(block, spans), shared * HDIM : (shared + 1) * HDIM],
            (((1,), (1,)), ((), ())),
            preferred_element_type=jnp.float32,
        )
        if masked:
            seen = (spans - PART) * SPAN
            row = lax.broadcasted_iota(jnp.int32, (rows, PART * SPAN), 0) % tall
            column = lax.broadcasted_iota(jnp.int32, (rows, PART * SPAN), 1)
            last = jnp.where(column <= row + edge, found[:, seen:], -jnp.inf)
            found = jnp.concatenate([found[:, :seen], last], axis=1) if seen else last
        return found

    def products(shared, block, spans, found):
        return jnp.dot(
            jnp.exp2(found * scale).astype(jnp.bfloat16),
            wide_ref[keys_of(block, spans), 2 * shared * HDIM : 2 * (shared + 1) * HDIM],
            preferred_element_type=jnp.float32,
        )

    def add(block, carry):
        found = [scores(shared, block, BLOCK, False) for shared in heads]
        for shared in heads:
            before = jnp.where(block > 0, mixed[shared], 0.0)
            mixed[shared] = before + products(shared, block, BLOCK, found[shared])
        return carry

    most = k_ref.shape[0] // SPAN
    if most > BLOCK:
        lax.fori_loop(0, blocks, add, 0)
    for spans in range(PART, min(BLOCK, most) + 1, PART):

        @pl.when(span % BLOCK // PART == spans // PART - 1)
        def _(spans=spans):
            found = [scores(shared, blocks, spans, True) for shared in heads]
            for shared in heads:
                before = jnp.where(blocks > 0, mixed[shared], 0.0)
                whole = before + products(shared, blocks, spans, found[shared])
                divide(whole, shared, o_ref, bounds)


def attend_piece_shifted(span, start, stacked, k_ref, wide_ref, mixed, o_ref, bounds, top):
    kv_heads, rows, _ = stacked.shape
    tall = o_ref.shape[0]
    scale = LOG2E / math.sqrt(HDIM)

    def one_head(shared, carry):
        def scores(block):
            found = lax.dot_general(
                stacked[shared],
                k_ref[rows_of(block), pl.ds(pl.multiple_of(shared * HDIM, HDIM), HDIM)],
                (((1,), (1,)), ((), ())),
                preferred_element_type=jnp.float32,
            )
            row = lax.broadcasted_iota(jnp.int32, (rows, SPAN), 0) % tall
            column = lax.broadcasted_iota(jnp.int32, (rows, SPAN), 1)
            return jnp.where(column <= row + (span - block) * SPAN + start, found, -jnp.inf)

        def look(block, carry):
            top[...] = jnp.maximum(top[...], scores(block))
            return carry

        def add(block, carry):
            weights = jnp.exp2((scores(block) - top[...]) * scale).astype(jnp.bfloat16)
            mixed[shared] += jnp.dot(
                weights,
                wide_ref[
                    rows_of(block), pl.ds(pl.multiple_of(2 * shared * HDIM, 2 * HDIM), 2 * HDIM)
                ],
                preferred_element_type=jnp.float32,
            )
            return carry

        top[...] = jnp.full_like(top, -jnp.inf)
        lax.fori_loop(0, span + 1, look, 0)
        top[...] = jnp.broadcast_to(jnp.max(top[...], axis=1, keepdims=True), top.shape)
        mixed[shared] = jnp.zeros(mixed.shape[1:], mixed.dtype)
        lax.fori_loop(0, span + 1, add, 0)
        return carry

    lax.fori_loop(0, kv_heads, one_head, 0)
    for shared in range(kv_heads):
        divide(mixed[shared], shared, o_ref, bounds)


def twice_if_needed(work, drain, bounds):
    bounds[...] = jnp.ones_like(bounds)
    work(False)
    safe = (bounds[0] > LEAST_SUM) & (bounds[1] < MOST_SUM)
    unsafe = jnp.max(jnp.where(safe, 0.0, 1.0)) > 0.5
    drain()

    @pl.when(unsafe)
    def _():
        work(True)
        drain()


def work_space(count, tall, width, key_width):
    kv_heads = key_width // HDIM
    rows = width // key_width * tall
    return [
        pltpu.VMEM((count, kv_heads, rows, HDIM), jnp.bfloat16),
        pltpu.VMEM((kv_heads, rows, 2 * HDIM), jnp.float32),
        pltpu.VMEM((rows, HDIM), jnp.float32),
        pltpu.VMEM((2, 8, HDIM), jnp.float32),
    ]


def rows_of(span):
    return pl.ds(pl.multiple_of(span * SPAN, SPAN), SPAN)


def half_of(span, start):
    return pl.ds(pl.multiple_of(span * SPAN + start, SPAN // 2), SPAN // 2)


def pick(j, options):
    chosen = options[0]
    for n in range(1, len(options)):
        chosen = jnp.where(j == n, options[n], chosen)
    return chosen


def attend_pieces(dests, starts, q_refs, k_ref, wide_ref, out_buf, store, stacked, mixed, top, bounds):
    count = len(dests)
    for j in range(count):

        @pl.when(dests[j] >= 0)
        def _(j=j):
            stack(q_refs[j], stacked.at[j])

    def work(shifted):
        def one(j, carry):
            dest, start = pick(j, dests), pick(j, starts)

            @pl.when(dest >= 0)
            def _():
                args = (dest, start, stacked.at[j], k_ref, wide_ref, mixed, out_buf.at[j], bounds)
                if shifted:
                    attend_piece_shifted(*args, top)
                else:
                    attend_piece(*args)
                if store is not None:
                    store(j, dest, start).start()

            return carry

        lax.fori_loop(0, count, one, 0)

    def drain():
        if store is not None:
            for j in range(count):
                pl.when(dests[j] >= 0)(store(j, jnp.maximum(dests[j], 0), starts[j]).wait)

    twice_if_needed(work, drain, bounds)


def stores(buf, o_ref, sems):
    return lambda j, span, start: pltpu.make_async_copy(
        buf.at[j], o_ref.at[half_of(span, start)], sems.at[j]
    )


def local_kernel(length_ref, q_ref, k_ref, v_ref, out_buf, wide, *work):
    live = length_ref[lax.axis_index("replica")]
    widen(v_ref, wide)
    half = SPAN // 2
    second = jnp.where(live > 1, 1, -1)
    attend_pieces(
        [jnp.int32(0), jnp.int32(0), second, second],
        [0, half, 0, half],
        [q_ref.at[n * half : (n + 1) * half] for n in range(2 * SLOTS)],
        k_ref,
        wide,
        out_buf,
        None,
        *work,
    )


def attend_local(lengths, queries, keys, values):
    width, key_width = queries.shape[1], keys.shape[1]
    return pl.pallas_call(
        local_kernel,
        out_shape=jax.ShapeDtypeStruct((2 * SLOTS, SPAN // 2, width), queries.dtype),
        in_specs=[SMEM, VMEM, VMEM, VMEM],
        out_specs=VMEM,
        scratch_shapes=[
            pltpu.VMEM((SLOTS * SPAN, 2 * key_width), keys.dtype),
            *work_space(2 * SLOTS, SPAN // 2, width, key_width),
        ],
        compiler_params=pltpu.CompilerParams(vmem_limit_bytes=VMEM_BYTES),
        cost_estimate=cost_of(3.5),
    )(lengths, queries, keys, values)


def any_of(dests):
    return functools.reduce(jnp.maximum, dests) >= 0


def first_kernel(kv_offsets, places, meta_ref, own_k, own_v, *refs):
    blocks, refs = refs[: len(kv_offsets)], refs[len(kv_offsets) :]
    q_refs, refs = refs[: len(places)], refs[len(places) :]
    local, o_k, o_v, k_buf, wide, out_buf, o_ref, v_buf, zeros, out_sems, span_sems, *work = refs
    live = entry(meta_ref, 0)
    half = SPAN // 2
    kv_dests = entries(meta_ref, kv_offsets)

    def each_span(act):
        for span in range(MAXC):
            if span < SLOTS:
                for n in range(2):
                    copy = pltpu.make_async_copy(
                        local.at[2 * span + n],
                        o_ref.at[half_of(span, n * half)],
                        span_sems.at[span, n],
                    )
                    pl.when(span < live)(getattr(copy, act))
            if span > 0:
                copy = pltpu.make_async_copy(zeros, o_ref.at[rows_of(span)], span_sems.at[span, 0])
                pl.when(span >= live)(getattr(copy, act))

    zeros[...] = jnp.zeros_like(zeros)
    each_span("start")
    k_buf[rows_of(0), :] = own_k[:SPAN, :]
    v_buf[rows_of(0), :] = own_v[:SPAN, :]

    @pl.when(live > 1)
    def _():
        k_buf[rows_of(1), :] = own_k[SPAN:, :]
        v_buf[rows_of(1), :] = own_v[SPAN:, :]

    for span in range(1, MAXC):

        @pl.when(span >= live)
        def _(span=span):
            k_buf[rows_of(span), :] = jnp.zeros((SPAN, k_buf.shape[1]), k_buf.dtype)
            v_buf[rows_of(span), :] = jnp.zeros((SPAN, v_buf.shape[1]), v_buf.dtype)

    for block, dest in zip(blocks, kv_dests, strict=True):

        @pl.when(dest >= 0)
        def _(block=block, dest=dest):
            k_buf[rows_of(dest), :] = block[:SPAN, :]
            v_buf[rows_of(dest), :] = block[SPAN:, :]

    copy_k = pltpu.make_async_copy(k_buf, o_k, out_sems.at[0])
    copy_v = pltpu.make_async_copy(v_buf, o_v, out_sems.at[1])
    copy_k.start()
    copy_v.start()
    dests = entries(meta_ref, [offset for offset, _ in places])

    @pl.when(live > 1)
    def _():
        widen(v_buf, wide)

    @pl.when(any_of(dests))
    def _():
        starts = [start for _, start in places]
        attend_pieces(dests, starts, q_refs, k_buf, wide, out_buf, None, *work)

    copy_k.wait()
    copy_v.wait()
    each_span("wait")


def attend_first(meta, keys, values, kv_offsets, kv_blocks, pieces, local):
    rows, key_width = MAXC * SPAN, keys.shape[1]
    queries = [piece[0] for piece in pieces]
    places = [piece[1:] for piece in pieces]
    count, (tall, width) = len(pieces), queries[0].shape
    out = jax.ShapeDtypeStruct((rows, key_width), keys.dtype)
    return pl.pallas_call(
        lambda *refs: first_kernel(kv_offsets, places, *refs),
        out_shape=(
            out,
            out,
            out,
            jax.ShapeDtypeStruct((rows, 2 * key_width), keys.dtype),
            jax.ShapeDtypeStruct((count, tall, width), keys.dtype),
            jax.ShapeDtypeStruct((rows, width), keys.dtype),
        ),
        in_specs=[VMEM] * (len(kv_blocks) + count + 4),
        out_specs=(ANY, ANY, VMEM, VMEM, VMEM, ANY),
        scratch_shapes=[
            pltpu.VMEM((rows, key_width), keys.dtype),
            pltpu.VMEM((SPAN, width), keys.dtype),
            pltpu.SemaphoreType.DMA((2,)),
            pltpu.SemaphoreType.DMA((MAXC, 2)),
            *work_space(count, tall, width, key_width),
        ],
        compiler_params=pltpu.CompilerParams(vmem_limit_bytes=VMEM_BYTES),
        cost_estimate=cost_of(2 + 1.3 * count),
    )(meta, keys, values, *kv_blocks, *queries, local)


def later_kernel(places, meta_ref, *refs):
    q_refs, (k_ref, wide_ref, out_buf, *work) = refs[: len(places)], refs[len(places) :]
    dests = entries(meta_ref, [offset for offset, _ in places])

    @pl.when(any_of(dests))
    def _():
        starts = [start for _, start in places]
        attend_pieces(dests, starts, q_refs, k_ref, wide_ref, out_buf, None, *work)


def attend_later(meta, pieces, ordered_keys, wide_values):
    queries = [piece[0] for piece in pieces]
    places = [piece[1:] for piece in pieces]
    count, (tall, width) = len(pieces), queries[0].shape
    return pl.pallas_call(
        lambda *refs: later_kernel(places, *refs),
        out_shape=jax.ShapeDtypeStruct((count, tall, width), ordered_keys.dtype),
        in_specs=[VMEM] * (count + 3),
        out_specs=VMEM,
        scratch_shapes=work_space(count, tall, width, ordered_keys.shape[1]),
        compiler_params=pltpu.CompilerParams(vmem_limit_bytes=VMEM_BYTES),
        cost_estimate=cost_of(1 + 1.3 * count),
    )(meta, *queries, ordered_keys, wide_values)


def last_kernel(before, places, meta_ref, *refs):
    results, refs = refs[: len(before)], refs[len(before) :]
    q_refs, refs = refs[: len(places)], refs[len(places) :]
    k_ref, wide_ref, _, o_ref, out_buf, sems, out_sems, *work = refs
    known = {
        offset: entry(meta_ref, offset) for its_places in before for offset, _ in its_places
    }

    def each(act):
        for n, (result, its_places) in enumerate(zip(results, before, strict=True)):
            for j, (offset, start) in enumerate(its_places):
                dest = known[offset]
                copy = pltpu.make_async_copy(
                    result.at[j], o_ref.at[half_of(jnp.maximum(dest, 0), start)], sems.at[n, j]
                )
                pl.when(dest >= 0)(getattr(copy, act))

    each("start")
    dests = entries(meta_ref, [offset for offset, _ in places])

    @pl.when(any_of(dests))
    def _():
        starts = [start for _, start in places]
        store = stores(out_buf, o_ref, out_sems)
        attend_pieces(dests, starts, q_refs, k_ref, wide_ref, out_buf, store, *work)

    each("wait")


def attend_last(meta, before, results, pieces, ordered_keys, wide_values, attention):
    queries = [piece[0] for piece in pieces]
    places = [piece[1:] for piece in pieces]
    count, (tall, width) = len(pieces), queries[0].shape
    most = max([1, *(len(its_places) for its_places in before)])
    return pl.pallas_call(
        lambda *refs: last_kernel(before, places, *refs),
        out_shape=jax.ShapeDtypeStruct(attention.shape, attention.dtype),
        in_specs=[VMEM] * (len(results) + count + 3) + [ANY],
        out_specs=ANY,
        input_output_aliases={len(results) + count + 3: 0},
        scratch_shapes=[
            pltpu.VMEM((count, tall, width), attention.dtype),
            pltpu.SemaphoreType.DMA((max(1, len(before)), most)),
            pltpu.SemaphoreType.DMA((count,)),
            *work_space(count, tall, width, ordered_keys.shape[1]),
        ],
        compiler_params=pltpu.CompilerParams(vmem_limit_bytes=VMEM_BYTES),
        cost_estimate=cost_of(2.5),
    )(meta, *results, *queries, ordered_keys, wide_values, attention)


def gathered_kernel(meta_ref, first_ref, later_ref, k_ref, v_ref, o_ref, wide, stacked, mixed, top, bounds):
    at = pl.program_id(1)
    live = meta_ref[0]
    widen(v_ref, wide)

    @pl.when(at == 0)
    def _():
        stack(first_ref, stacked.at[0])

    @pl.when(at > 0)
    def _():
        stack(later_ref.at[0], stacked.at[0])

    def work(shifted):
        args = (at, 0, stacked.at[0], k_ref, wide, mixed, o_ref, bounds)
        if shifted:
            attend_piece_shifted(*args, top)
        else:
            attend_piece(*args)

    @pl.when(at < live)
    def _():
        twice_if_needed(work, lambda: None, bounds)

    @pl.when(at >= live)
    def _():
        o_ref[...] = jnp.zeros_like(o_ref)


def attend_gathered(live, source, first, later, cache_keys, cache_values):
    home_rows, key_width = cache_keys.shape
    width = first.shape[1]
    groups = key_width // HDIM
    part = width // groups
    meta = jnp.concatenate([live.reshape(1), source]).astype(jnp.int32)
    return pl.pallas_call(
        gathered_kernel,
        out_shape=jax.ShapeDtypeStruct((home_rows, width), first.dtype),
        grid_spec=pltpu.PrefetchScalarGridSpec(
            num_scalar_prefetch=1,
            grid=(groups, MAXC),
            in_specs=[
                pl.BlockSpec((SPAN, part), lambda g, m, meta: (0, g)),
                pl.BlockSpec((1, SPAN, part), lambda g, m, meta: (meta[1 + m], 0, g)),
                pl.BlockSpec((home_rows, HDIM), lambda g, m, meta: (0, g)),
                pl.BlockSpec((home_rows, HDIM), lambda g, m, meta: (0, g)),
            ],
            out_specs=pl.BlockSpec((SPAN, part), lambda g, m, meta: (m, g)),
            scratch_shapes=[
                pltpu.VMEM((home_rows, 2 * HDIM), cache_keys.dtype),
                *work_space(1, SPAN, part, HDIM),
            ],
        ),
        compiler_params=pltpu.CompilerParams(vmem_limit_bytes=VMEM_BYTES),
    )(meta, first, later, cache_keys, cache_values)


def gather_all(queries, keys, values, lengths, slot_prompt, slot_span):
    mine = lax.axis_index("replica")
    home_rows, key_width = MAXC * SPAN, keys.shape[1]
    live = lengths[mine]
    spans = jnp.arange(MAXC, dtype=jnp.int32)
    matches = (slot_prompt[None, :, 1] == mine) & (slot_span[None, :, 1] == spans[:, None])
    here = jnp.any(matches, axis=1)
    source = jnp.argmax(matches, axis=1).astype(jnp.int32)
    slots_k = lax.all_gather(keys[SPAN:], "replica")
    slots_v = lax.all_gather(values[SPAN:], "replica")
    slots_q = lax.all_gather(queries[SPAN:], "replica")

    def in_order(first, slots):
        picked = jnp.take(slots, source, axis=0)
        kept = jnp.where(here[:, None, None], picked, jnp.zeros((), slots.dtype))
        return jnp.concatenate([first, kept[1:].reshape(home_rows - SPAN, key_width)], axis=0)

    cache_keys = in_order(keys[:SPAN], slots_k)
    cache_values = in_order(values[:SPAN], slots_v)
    attention = attend_gathered(live, source, queries[:SPAN], slots_q, cache_keys, cache_values)
    return (attention, cache_keys, cache_values)


def per_device(queries, keys, values, lengths, slot_prompt, slot_span):
    replicas = lax.axis_size("replica")
    if replicas != 8:
        return gather_all(queries, keys, values, lengths, slot_prompt, slot_span)
    ring = column_ring(replicas)
    farthest = replicas // 2

    def after(block, *others):
        return lax.optimization_barrier((block, others))[0]

    def joined(both):
        return list(lax.optimization_barrier(tuple(both)))

    def shift(block, step):
        pairs = [(r, ring[(n + step) % replicas]) for n, r in enumerate(ring)]
        return lax.ppermute(block, "replica", pairs)

    def go_on(both):
        return [shift(both[0], 1), shift(both[1], -1)]

    own_kv = pack_kv(keys, values)
    kv = [[own_kv, own_kv]]
    kv.append(go_on(kv[0]))
    own_top, own_bottom = pack_q(after(queries, own_kv))
    first, second = [[own_top, own_bottom]], [[own_bottom, own_top]]
    first.append(joined(go_on(first[0])))
    kv[1] = joined(kv[1])
    kv.append(joined(go_on(kv[1])))
    local = attend_local(lengths, after(queries, kv[1]), keys, values)
    second.append(joined(go_on([after(block, first[1]) for block in second[0]])))
    kv.append(joined(go_on([after(block, local) for block in kv[2]])))
    first.append(joined(go_on([after(block, kv[3]) for block in first[1]])))
    kv.append([shift(kv[3][0], 1)])
    second.append(joined(go_on([after(block, kv[3]) for block in second[1]])))
    meta = places(lengths, slot_prompt, slot_span)
    offsets = [[n, replicas - n] for n in range(1, farthest)]

    def wave(n, which):
        up, down = offsets[n - 1]
        if which is first:
            return [(first[n][0], up, 0), (first[n][1], down, half)]
        return [(second[n][0], up, half), (second[n][1], down, 0)]

    half = SPAN // 2
    cache_keys, cache_values, ordered_keys, wide_values, result, attention = attend_first(
        meta,
        keys,
        values,
        sum(offsets, []) + [farthest],
        sum(kv[1:], []),
        wave(1, first) + wave(1, second),
        local,
    )
    results, before = [result], [wave(1, first) + wave(1, second)]

    def attend(n, which):
        results.append(attend_later(meta, wave(n, which), ordered_keys, wide_values))
        before.append(wave(n, which))

    first.append(joined(go_on(first[2])))
    attend(2, first)
    second.append(joined(go_on([after(block, results[-1]) for block in second[2]])))
    attend(2, second)
    last = [
        (shift(after(first[3][0], results[-1]), 1), farthest, 0),
        (shift(after(first[3][1], results[-1]), -1), farthest, half),
    ]
    attend(3, first)
    attend(3, second)
    before = [[piece[1:] for piece in pieces] for pieces in before]
    attention = attend_last(
        meta, before, results, last[1:], ordered_keys, wide_values, attention
    )
    attention = attend_last(meta, [], [], last[:1], ordered_keys, wide_values, attention)
    return (attention, cache_keys, cache_values)


def solution(mesh):
    in_specs = (
        P(("group", "replica"), "tensor"),
        P(("group", "replica"), "tensor"),
        P(("group", "replica"), "tensor"),
        P("group"),
        P("group", None),
        P("group", None),
    )
    out_specs = (
        P(("group", "replica"), "tensor"),
        P(("group", "replica"), "tensor"),
        P(("group", "replica"), "tensor"),
    )
    return jax.shard_map(
        per_device, mesh=mesh, in_specs=in_specs, out_specs=out_specs, check_vma=False
    )
```

profile of v0, /device:TPU:0, one launch (start us, length us, event | category | flops | bytes accessed | tf_op | source)
XLA Modules:
  0.0 153.9 jit_solution(13638981355071658217)
XLA Ops:
  0.6 0.0 copy-start.3
  0.6 0.0 copy-start.2
  0.7 0.0 copy-start.1
  0.7 0.0 copy-start.4
  0.7 0.0 copy-start.5
  0.7 0.0 copy-start
  0.7 1.6 %shard_map.85 = bf16[256,256]{1,0:T(8,128)(2,1)} custom-call(bf16[256,256]{1,0:T(8,128)(2,1)} %refs_1_.1, bf16[256,256]{1,0:T(8,128)(2,1)} %refs_2_.1), custom_call_target="tpu_custom_call" | custom-call | flops 1150000000 | tf_op jit(solution)/shard_map/pallas_call | solution.py:52
  2.3 3.0 %collective-permute-start.3 = (bf16[256,256]{1,0:T(8,128)(2,1)}, bf16[256,256]{1,0:T(8,128)(2,1)S(1)}, u32[]{:S(2)}, u32[]{:S(2)}) collective-permute-start(bf16[256,256]{1,0:T(8,128)(2,1)} %shard_map.85), channel_id=1, source_target_pairs={{0,2},{4,0},{8,4},{12,8},{14,12},{10,14},{6,10},{2,6},{1,3},{5,1},... | collective-permute-start | bytes 393224 | tf_op jit(solution)/shard_map/ppermute | solution.py:624
  5.3 0.1 collective-permute-start.2
  5.5 0.0 copy-done.1
  5.5 0.1 shard_map.86
  5.5 2.0 %collective-permute-start = (bf16[64,2048]{1,0:T(8,128)(2,1)S(1)}, bf16[64,2048]{1,0:T(8,128)(2,1)S(1)}, u32[]{:S(2)}, u32[]{:S(2)}) collective-permute-start(bf16[64,2048]{1,0:T(8,128)(2,1)S(1)} %get-tuple-element.63), channel_id=1, source_target_pairs={{0,4},{4,8},{8,12},{12,14},{14,10},{10,6},{6,2},{2,0},{1,5},{5,9},... | collective-permute-start | bytes 786440 | tf_op jit(solution)/shard_map/ppermute | solution.py:624
  7.6 0.1 collective-permute-start.1
  7.6 0.0 copy-done.4
  7.6 0.0 copy-done.5
  7.7 0.0 copy-done
  7.7 1.8 %collective-permute-done.3.refs_4_ = bf16[256,256]{1,0:T(8,128)(2,1)S(1)} collective-permute-done((bf16[256,256]{1,0:T(8,128)(2,1)}, bf16[256,256]{1,0:T(8,128)(2,1)S(1)}, u32[]{:S(2)}, u32[]{:S(2)}) %collective-permute-start.3) | collective-permute-done | bytes 131104 | tf_op jit(solution)/shard_map/ppermute | solution.py:624
  9.5 2.4 %collective-permute-done.2.refs_3_ = bf16[256,256]{1,0:T(8,128)(2,1)S(1)} collective-permute-done((bf16[256,256]{1,0:T(8,128)(2,1)}, bf16[256,256]{1,0:T(8,128)(2,1)S(1)}, u32[]{:S(2)}, u32[]{:S(2)}) %collective-permute-start.2) | collective-permute-done | bytes 131104 | tf_op jit(solution)/shard_map/ppermute | solution.py:624
  12.0 0.1 collective-permute-start.4
  12.1 1.9 %collective-permute-start.5 = (bf16[256,256]{1,0:T(8,128)(2,1)S(1)}, bf16[256,256]{1,0:T(8,128)(2,1)S(1)}, u32[]{:S(2)}, u32[]{:S(2)}) collective-permute-start(bf16[256,256]{1,0:T(8,128)(2,1)S(1)} %collective-permute-done.3.refs_4_), channel_id=1, source_target_pairs={{0,2},{4,0},{8,4},{12,8},{14,12},{10,14},{6,10},{2,6},{1,3},{5,1},... | collective-permute-start | bytes 393224 | tf_op jit(solution)/shard_map/ppermute | solution.py:624
  14.0 12.3 %shard_map.87.refs_14_ = bf16[4,64,2048]{2,1,0:T(8,128)(2,1)S(1)} custom-call(s32[8]{0:T(128)S(1)} %copy-done, bf16[256,2048]{1,0:T(8,128)(2,1)S(1)} %copy-done.1, bf16[256,256]{1,0:T(8,128)(2,1)S(1)} %copy-done.2, bf16[256,256]{1,0:T(8,128)(2,1)S(1)} %copy-done.3), custom_call_target="tpu_custom_call" | custom-call | flops 4024999936 | tf_op jit(solution)/shard_map/pallas_call | solution.py:339
  26.3 0.0 collective-permute-done.4.refs_5_
  26.3 0.0 collective-permute-done.5.refs_6_
  26.3 0.1 collective-permute-start.6
  26.4 2.0 %collective-permute-start.7 = (bf16[256,256]{1,0:T(8,128)(2,1)S(1)}, bf16[256,256]{1,0:T(8,128)(2,1)S(1)}, u32[]{:S(2)}, u32[]{:S(2)}) collective-permute-start(bf16[256,256]{1,0:T(8,128)(2,1)S(1)} %collective-permute-done.5.refs_6_), channel_id=1, source_target_pairs={{0,2},{4,0},{8,4},{12,8},{14,12},{10,14},{6,10},{2,6},{1,3},{5,1},... | collective-permute-start | bytes 393224 | tf_op jit(solution)/shard_map/ppermute | solution.py:624
  28.4 0.0 collective-permute-done.refs_10_
  28.4 0.0 collective-permute-done.1.refs_11_
  28.4 0.1 collective-permute-start.12
  28.5 2.0 %collective-permute-start.13 = (bf16[64,2048]{1,0:T(8,128)(2,1)S(1)}, bf16[64,2048]{1,0:T(8,128)(2,1)S(1)}, u32[]{:S(2)}, u32[]{:S(2)}) collective-permute-start(bf16[64,2048]{1,0:T(8,128)(2,1)S(1)} %get-tuple-element.63), channel_id=1, source_target_pairs={{0,2},{4,0},{8,4},{12,8},{14,12},{10,14},{6,10},{2,6},{1,3},{5,1},... | collective-permute-start | bytes 786440 | tf_op jit(solution)/shard_map/ppermute | solution.py:624
  30.5 0.2 add_reduce_fusion
  30.7 2.1 %collective-permute-done.6.refs_7_ = bf16[256,256]{1,0:T(8,128)(2,1)S(1)} collective-permute-done((bf16[256,256]{1,0:T(8,128)(2,1)S(1)}, bf16[256,256]{1,0:T(8,128)(2,1)S(1)}, u32[]{:S(2)}, u32[]{:S(2)}) %collective-permute-start.6) | collective-permute-done | bytes 131104 | tf_op jit(solution)/shard_map/ppermute | solution.py:624
  32.8 0.0 collective-permute-done.7.refs_8_
  32.8 0.0 collective-permute-start.16
  32.8 0.1 collective-permute-start.8
  32.9 2.0 %collective-permute-start.9 = (bf16[64,2048]{1,0:T(8,128)(2,1)S(1)}, bf16[64,2048]{1,0:T(8,128)(2,1)S(1)}, u32[]{:S(2)}, u32[]{:S(2)}) collective-permute-start(bf16[64,2048]{1,0:T(8,128)(2,1)S(1)} %collective-permute-done.1.refs_11_), channel_id=1, source_target_pairs={{0,2},{4,0},{8,4},{12,8},{14,12},{10,14},{6,10},{2,6},{1,3},{5,1},... | collective-permute-start | bytes 786440 | tf_op jit(solution)/shard_map/ppermute | solution.py:624
  34.9 3.5 %collective-permute-done.12.refs_12_ = bf16[64,2048]{1,0:T(8,128)(2,1)S(1)} collective-permute-done((bf16[64,2048]{1,0:T(8,128)(2,1)S(1)}, bf16[64,2048]{1,0:T(8,128)(2,1)S(1)}, u32[]{:S(2)}, u32[]{:S(2)}) %collective-permute-start.12) | collective-permute-done | bytes 262176 | tf_op jit(solution)/shard_map/ppermute | solution.py:624
  38.4 0.0 collective-permute-done.13.refs_13_
  38.4 0.0 collective-permute-start.14
  38.4 2.0 %collective-permute-start.15 = (bf16[64,2048]{1,0:T(8,128)(2,1)S(1)}, bf16[64,2048]{1,0:T(8,128)(2,1)S(1)}, u32[]{:S(2)}, u32[]{:S(2)}) collective-permute-start(bf16[64,2048]{1,0:T(8,128)(2,1)S(1)} %collective-permute-done.13.refs_13_), channel_id=1, source_target_pairs={{0,2},{4,0},{8,4},{12,8},{14,12},{10,14},{6,10},{2,6},{1,3},{5,1},... | collective-permute-start | bytes 786440 | tf_op jit(solution)/shard_map/ppermute | solution.py:624
  40.4 0.8 collective-permute-done.16.refs_9_
  41.2 0.1 broadcast_in_dim.32.refs_0_
  41.3 31.8 %shard_map.88 = (bf16[1024,256]{1,0:T(8,128)(2,1)}, bf16[1024,256]{1,0:T(8,128)(2,1)}, bf16[1024,256]{1,0:T(8,128)(2,1)S(1)}, bf16[1024,512]{1,0:T(8,128)(2,1)S(...) custom-call(s32[8,128]{1,0:T(8,128)S(1)} %broadcast_in_dim.32.refs_0_, bf16[256,256]{1,0:T(8,128)(2,1)S(1)} %copy-done.2, ...), custom_call_target="tpu_custom_call" | custom-call | flops 8280000000 | tf_op jit(solution)/shard_map/pallas_call | solution.py:429
  73.1 0.0 collective-permute-done.8.refs_1_
  73.1 0.0 collective-permute-done.9.refs_2_
  73.1 0.1 collective-permute-start.10
  73.2 2.0 %collective-permute-start.11 = (bf16[64,2048]{1,0:T(8,128)(2,1)S(1)}, bf16[64,2048]{1,0:T(8,128)(2,1)S(1)}, u32[]{:S(2)}, u32[]{:S(2)}) collective-permute-start(bf16[64,2048]{1,0:T(8,128)(2,1)S(1)} %collective-permute-done.9.refs_2_), channel_id=1, source_target_pairs={{0,2},{4,0},{8,4},{12,8},{14,12},{10,14},{6,10},{2,6},{1,3},{5,1},... | collective-permute-start | bytes 786440 | tf_op jit(solution)/shard_map/ppermute | solution.py:624
  75.2 18.2 %shard_map.90.refs_2_ = bf16[2,64,2048]{2,1,0:T(8,128)(2,1)S(1)} custom-call(s32[8,128]{1,0:T(8,128)S(1)} %broadcast_in_dim.32.refs_0_, bf16[64,2048]{1,0:T(8,128)(2,1)S(1)} %collective-permute-done.8.refs_1_, bf16[64,2048]{1,0:T(8,128)(2,1)S(1)} %collective-permute-done.9.refs_2_, bf16[1024,256]{1,0:T(8,128)(2,1)S(1)} %get-tuple-element.70.refs_3_.refs_7_.refs_2_, ...), custom_call_target="tpu_custom_call" | custom-call | flops 4140000000 | tf_op jit(solution)/shard_map/pallas_call | solution.py:467
  93.4 0.0 collective-permute-done.14.refs_1_
  93.4 0.0 collective-permute-done.15.refs_2_
  93.4 0.1 collective-permute-start.18
  93.5 2.0 %collective-permute-start.19 = (bf16[64,2048]{1,0:T(8,128)(2,1)S(1)}, bf16[64,2048]{1,0:T(8,128)(2,1)S(1)}, u32[]{:S(2)}, u32[]{:S(2)}) collective-permute-start(bf16[64,2048]{1,0:T(8,128)(2,1)S(1)} %collective-permute-done.15.refs_2_), channel_id=1, source_target_pairs={{0,2},{4,0},{8,4},{12,8},{14,12},{10,14},{6,10},{2,6},{1,3},{5,1},... | collective-permute-start | bytes 786440 | tf_op jit(solution)/shard_map/ppermute | solution.py:624
  95.5 18.2 %shard_map.89.refs_3_ = bf16[2,64,2048]{2,1,0:T(8,128)(2,1)S(1)} custom-call(s32[8,128]{1,0:T(8,128)S(1)} %broadcast_in_dim.32.refs_0_, bf16[64,2048]{1,0:T(8,128)(2,1)S(1)} %collective-permute-done.14.refs_1_, bf16[64,2048]{1,0:T(8,128)(2,1)S(1)} %collective-permute-done.15.refs_2_, bf16[1024,256]{1,0:T(8,128)(2,1)S(1)} %get-tuple-element.70.refs_3_.refs_7_.refs_2_, ...), custom_call_target="tpu_custom_call" | custom-call | flops 4140000000 | tf_op jit(solution)/shard_map/pallas_call | solution.py:467
  113.7 0.0 collective-permute-done.10.refs_1_
  113.7 0.0 collective-permute-done.11.refs_2_
  113.7 0.1 collective-permute-start.17
  113.8 2.0 %collective-permute-start.20 = (bf16[64,2048]{1,0:T(8,128)(2,1)S(1)}, bf16[64,2048]{1,0:T(8,128)(2,1)S(1)}, u32[]{:S(2)}, u32[]{:S(2)}) collective-permute-start(bf16[64,2048]{1,0:T(8,128)(2,1)S(1)} %collective-permute-done.11.refs_2_), channel_id=1, source_target_pairs={{0,2},{4,0},{8,4},{12,8},{14,12},{10,14},{6,10},{2,6},{1,3},{5,1},... | collective-permute-start | bytes 786440 | tf_op jit(solution)/shard_map/ppermute | solution.py:624
  115.8 9.4 %shard_map.91.refs_4_ = bf16[2,64,2048]{2,1,0:T(8,128)(2,1)S(1)} custom-call(s32[8,128]{1,0:T(8,128)S(1)} %broadcast_in_dim.32.refs_0_, bf16[64,2048]{1,0:T(8,128)(2,1)S(1)} %collective-permute-done.10.refs_1_, bf16[64,2048]{1,0:T(8,128)(2,1)S(1)} %collective-permute-done.11.refs_2_, bf16[1024,256]{1,0:T(8,128)(2,1)S(1)} %get-tuple-element.70.refs_3_.refs_7_.refs_2_, ...), custom_call_target="tpu_custom_call" | custom-call | flops 4140000000 | tf_op jit(solution)/shard_map/pallas_call | solution.py:467
  125.1 0.0 collective-permute-done.18.refs_1_
  125.2 0.0 collective-permute-done.19.refs_2_
  125.2 9.4 %shard_map.92.refs_5_ = bf16[2,64,2048]{2,1,0:T(8,128)(2,1)S(1)} custom-call(s32[8,128]{1,0:T(8,128)S(1)} %broadcast_in_dim.32.refs_0_, bf16[64,2048]{1,0:T(8,128)(2,1)S(1)} %collective-permute-done.18.refs_1_, bf16[64,2048]{1,0:T(8,128)(2,1)S(1)} %collective-permute-done.19.refs_2_, bf16[1024,256]{1,0:T(8,128)(2,1)S(1)} %get-tuple-element.70.refs_3_.refs_7_.refs_2_, ...), custom_call_target="tpu_custom_call" | custom-call | flops 4140000000 | tf_op jit(solution)/shard_map/pallas_call | solution.py:467
  134.5 0.0 collective-permute-done.20.refs_6_
  134.5 9.7 %shard_map.93.refs_4_ = bf16[1024,2048]{1,0:T(8,128)(2,1)} custom-call(s32[8,128]{1,0:T(8,128)S(1)} %broadcast_in_dim.32.refs_0_, bf16[4,64,2048]{2,1,0:T(8,128)(2,1)S(1)} %get-tuple-element.73.refs_1_, bf16[2,64,2048]{2,1,0:T(8,128)(2,1)S(1)} %shard_map.90.refs_2_, bf16[2,64,2048]{2,1,0:T(8,128)(2,1)S(1)} %shard_map.89.refs_3_, ...), custom_call_target="tpu_custom_call", output_to_operand_aliasing={{}: (9, {})} | custom-call | flops 2875000064 | tf_op jit(solution)/shard_map/pallas_call | solution.py:512
  144.3 0.0 collective-permute-done.17.refs_1_
  144.3 9.4 %shard_map.94 = bf16[1024,2048]{1,0:T(8,128)(2,1)} custom-call(s32[8,128]{1,0:T(8,128)S(1)} %broadcast_in_dim.32.refs_0_, bf16[64,2048]{1,0:T(8,128)(2,1)S(1)} %collective-permute-done.17.refs_1_, bf16[1024,256]{1,0:T(8,128)(2,1)S(1)} %get-tuple-element.70.refs_3_.refs_7_.refs_2_, ...), custom_call_target="tpu_custom_call", output_to_operand_aliasing={{}: (4, {})} | custom-call | flops 2875000064 | tf_op jit(solution)/shard_map/pallas_call | solution.py:512
  (7 shorter events, 0.0 us)
Async XLA Ops:
  0.6 13.4 %copy-start.3 = (bf16[256,256]{1,0:T(8,128)(2,1)S(1)}, bf16[256,256]{1,0:T(8,128)(2,1)}, u32[]{:S(2)}) copy-start(bf16[256,256]{1,0:T(8,128)(2,1)} %refs_2_.1) | copy-start | bytes 393220
  0.6 13.4 %copy-start.2 = (bf16[256,256]{1,0:T(8,128)(2,1)S(1)}, bf16[256,256]{1,0:T(8,128)(2,1)}, u32[]{:S(2)}) copy-start(bf16[256,256]{1,0:T(8,128)(2,1)} %refs_1_.1) | copy-start | bytes 393220
  0.7 4.8 %copy-start.1 = (bf16[256,2048]{1,0:T(8,128)(2,1)S(1)}, bf16[256,2048]{1,0:T(8,128)(2,1)}, u32[]{:S(2)}) copy-start(bf16[256,2048]{1,0:T(8,128)(2,1)} %q_ref.1) | copy-start | bytes 3145732
  0.7 7.0 %copy-start.4 = (s32[8,2]{0,1:T(2,128)S(1)}, s32[8,2]{0,1:T(2,128)}, u32[]{:S(2)}) copy-start(s32[8,2]{0,1:T(2,128)} %param.10) | copy-start | bytes 196
  0.7 7.0 %copy-start.5 = (s32[8,2]{0,1:T(2,128)S(1)}, s32[8,2]{0,1:T(2,128)}, u32[]{:S(2)}) copy-start(s32[8,2]{0,1:T(2,128)} %param.11) | copy-start | bytes 196
  0.7 7.0 %copy-start = (s32[8]{0:T(128)S(1)}, s32[8]{0:T(128)}, u32[]{:S(2)}) copy-start(s32[8]{0:T(128)} %length_ref.1) | copy-start | bytes 100
  2.3 7.2 %collective-permute-start.3 = (bf16[256,256]{1,0:T(8,128)(2,1)}, bf16[256,256]{1,0:T(8,128)(2,1)S(1)}, u32[]{:S(2)}, u32[]{:S(2)}) collective-permute-start(bf16[256,256]{1,0:T(8,128)(2,1)} %shard_map.85), channel_id=1, source_target_pairs={{0,2},{4,0},{8,4},{12,8},{14,12},{10,14},{6,10},{2,6},{1,3},{5,1},... | collective-permute-start | bytes 393224 | tf_op jit(solution)/shard_map/ppermute | solution.py:624
  5.3 6.6 %collective-permute-start.2 = (bf16[256,256]{1,0:T(8,128)(2,1)}, bf16[256,256]{1,0:T(8,128)(2,1)S(1)}, u32[]{:S(2)}, u32[]{:S(2)}) collective-permute-start(bf16[256,256]{1,0:T(8,128)(2,1)} %shard_map.85), channel_id=1, source_target_pairs={{0,4},{4,8},{8,12},{12,14},{14,10},{10,6},{6,2},{2,0},{1,5},{5,9},... | collective-permute-start | bytes 393224 | tf_op jit(solution)/shard_map/ppermute | solution.py:624
  5.5 22.8 %collective-permute-start = (bf16[64,2048]{1,0:T(8,128)(2,1)S(1)}, bf16[64,2048]{1,0:T(8,128)(2,1)S(1)}, u32[]{:S(2)}, u32[]{:S(2)}) collective-permute-start(bf16[64,2048]{1,0:T(8,128)(2,1)S(1)} %get-tuple-element.63), channel_id=1, source_target_pairs={{0,4},{4,8},{8,12},{12,14},{14,10},{10,6},{6,2},{2,0},{1,5},{5,9},... | collective-permute-start | bytes 786440 | tf_op jit(solution)/shard_map/ppermute | solution.py:624
  7.6 20.8 %collective-permute-start.1 = (bf16[64,2048]{1,0:T(8,128)(2,1)S(1)}, bf16[64,2048]{1,0:T(8,128)(2,1)S(1)}, u32[]{:S(2)}, u32[]{:S(2)}) collective-permute-start(bf16[64,2048]{1,0:T(8,128)(2,1)S(1)} %get-tuple-element.62), channel_id=1, source_target_pairs={{0,2},{4,0},{8,4},{12,8},{14,12},{10,14},{6,10},{2,6},{1,3},{5,1},... | collective-permute-start | bytes 786440 | tf_op jit(solution)/shard_map/ppermute | solution.py:624
  12.0 14.3 %collective-permute-start.4 = (bf16[256,256]{1,0:T(8,128)(2,1)S(1)}, bf16[256,256]{1,0:T(8,128)(2,1)S(1)}, u32[]{:S(2)}, u32[]{:S(2)}) collective-permute-start(bf16[256,256]{1,0:T(8,128)(2,1)S(1)} %collective-permute-done.2.refs_3_), channel_id=1, source_target_pairs={{0,4},{4,8},{8,12},{12,14},{14,10},{10,6},{6,2},{2,0},{1,5},{5,9},... | collective-permute-start | bytes 393224 | tf_op jit(solution)/shard_map/ppermute | solution.py:624
  12.1 14.2 %collective-permute-start.5 = (bf16[256,256]{1,0:T(8,128)(2,1)S(1)}, bf16[256,256]{1,0:T(8,128)(2,1)S(1)}, u32[]{:S(2)}, u32[]{:S(2)}) collective-permute-start(bf16[256,256]{1,0:T(8,128)(2,1)S(1)} %collective-permute-done.3.refs_4_), channel_id=1, source_target_pairs={{0,2},{4,0},{8,4},{12,8},{14,12},{10,14},{6,10},{2,6},{1,3},{5,1},... | collective-permute-start | bytes 393224 | tf_op jit(solution)/shard_map/ppermute | solution.py:624
  26.3 6.5 %collective-permute-start.6 = (bf16[256,256]{1,0:T(8,128)(2,1)S(1)}, bf16[256,256]{1,0:T(8,128)(2,1)S(1)}, u32[]{:S(2)}, u32[]{:S(2)}) collective-permute-start(bf16[256,256]{1,0:T(8,128)(2,1)S(1)} %collective-permute-done.4.refs_5_), channel_id=1, source_target_pairs={{0,4},{4,8},{8,12},{12,14},{14,10},{10,6},{6,2},{2,0},{1,5},{5,9},... | collective-permute-start | bytes 393224 | tf_op jit(solution)/shard_map/ppermute | solution.py:624
  26.4 6.4 %collective-permute-start.7 = (bf16[256,256]{1,0:T(8,128)(2,1)S(1)}, bf16[256,256]{1,0:T(8,128)(2,1)S(1)}, u32[]{:S(2)}, u32[]{:S(2)}) collective-permute-start(bf16[256,256]{1,0:T(8,128)(2,1)S(1)} %collective-permute-done.5.refs_6_), channel_id=1, source_target_pairs={{0,2},{4,0},{8,4},{12,8},{14,12},{10,14},{6,10},{2,6},{1,3},{5,1},... | collective-permute-start | bytes 393224 | tf_op jit(solution)/shard_map/ppermute | solution.py:624
  28.4 10.0 %collective-permute-start.12 = (bf16[64,2048]{1,0:T(8,128)(2,1)S(1)}, bf16[64,2048]{1,0:T(8,128)(2,1)S(1)}, u32[]{:S(2)}, u32[]{:S(2)}) collective-permute-start(bf16[64,2048]{1,0:T(8,128)(2,1)S(1)} %get-tuple-element.62), channel_id=1, source_target_pairs={{0,4},{4,8},{8,12},{12,14},{14,10},{10,6},{6,2},{2,0},{1,5},{5,9},... | collective-permute-start | bytes 786440 | tf_op jit(solution)/shard_map/ppermute | solution.py:624
  28.5 9.9 %collective-permute-start.13 = (bf16[64,2048]{1,0:T(8,128)(2,1)S(1)}, bf16[64,2048]{1,0:T(8,128)(2,1)S(1)}, u32[]{:S(2)}, u32[]{:S(2)}) collective-permute-start(bf16[64,2048]{1,0:T(8,128)(2,1)S(1)} %get-tuple-element.63), channel_id=1, source_target_pairs={{0,2},{4,0},{8,4},{12,8},{14,12},{10,14},{6,10},{2,6},{1,3},{5,1},... | collective-permute-start | bytes 786440 | tf_op jit(solution)/shard_map/ppermute | solution.py:624
  32.8 8.4 %collective-permute-start.16 = (bf16[256,256]{1,0:T(8,128)(2,1)S(1)}, bf16[256,256]{1,0:T(8,128)(2,1)S(1)}, u32[]{:S(2)}, u32[]{:S(2)}) collective-permute-start(bf16[256,256]{1,0:T(8,128)(2,1)S(1)} %collective-permute-done.6.refs_7_), channel_id=1, source_target_pairs={{0,4},{4,8},{8,12},{12,14},{14,10},{10,6},{6,2},{2,0},{1,5},{5,9},... | collective-permute-start | bytes 393224 | tf_op jit(solution)/shard_map/ppermute | solution.py:624
  32.8 40.3 %collective-permute-start.8 = (bf16[64,2048]{1,0:T(8,128)(2,1)S(1)}, bf16[64,2048]{1,0:T(8,128)(2,1)S(1)}, u32[]{:S(2)}, u32[]{:S(2)}) collective-permute-start(bf16[64,2048]{1,0:T(8,128)(2,1)S(1)} %collective-permute-done.refs_10_), channel_id=1, source_target_pairs={{0,4},{4,8},{8,12},{12,14},{14,10},{10,6},{6,2},{2,0},{1,5},{5,9},... | collective-permute-start | bytes 786440 | tf_op jit(solution)/shard_map/ppermute | solution.py:624
  32.9 40.2 %collective-permute-start.9 = (bf16[64,2048]{1,0:T(8,128)(2,1)S(1)}, bf16[64,2048]{1,0:T(8,128)(2,1)S(1)}, u32[]{:S(2)}, u32[]{:S(2)}) collective-permute-start(bf16[64,2048]{1,0:T(8,128)(2,1)S(1)} %collective-permute-done.1.refs_11_), channel_id=1, source_target_pairs={{0,2},{4,0},{8,4},{12,8},{14,12},{10,14},{6,10},{2,6},{1,3},{5,1},... | collective-permute-start | bytes 786440 | tf_op jit(solution)/shard_map/ppermute | solution.py:624
  38.4 55.0 %collective-permute-start.14 = (bf16[64,2048]{1,0:T(8,128)(2,1)S(1)}, bf16[64,2048]{1,0:T(8,128)(2,1)S(1)}, u32[]{:S(2)}, u32[]{:S(2)}) collective-permute-start(bf16[64,2048]{1,0:T(8,128)(2,1)S(1)} %collective-permute-done.12.refs_12_), channel_id=1, source_target_pairs={{0,4},{4,8},{8,12},{12,14},{14,10},{10,6},{6,2},{2,0},{1,5},{5,9},... | collective-permute-start | bytes 786440 | tf_op jit(solution)/shard_map/ppermute | solution.py:624
  38.4 55.0 %collective-permute-start.15 = (bf16[64,2048]{1,0:T(8,128)(2,1)S(1)}, bf16[64,2048]{1,0:T(8,128)(2,1)S(1)}, u32[]{:S(2)}, u32[]{:S(2)}) collective-permute-start(bf16[64,2048]{1,0:T(8,128)(2,1)S(1)} %collective-permute-done.13.refs_13_), channel_id=1, source_target_pairs={{0,2},{4,0},{8,4},{12,8},{14,12},{10,14},{6,10},{2,6},{1,3},{5,1},... | collective-permute-start | bytes 786440 | tf_op jit(solution)/shard_map/ppermute | solution.py:624
  73.1 40.6 %collective-permute-start.10 = (bf16[64,2048]{1,0:T(8,128)(2,1)S(1)}, bf16[64,2048]{1,0:T(8,128)(2,1)S(1)}, u32[]{:S(2)}, u32[]{:S(2)}) collective-permute-start(bf16[64,2048]{1,0:T(8,128)(2,1)S(1)} %collective-permute-done.8.refs_1_), channel_id=1, source_target_pairs={{0,4},{4,8},{8,12},{12,14},{14,10},{10,6},{6,2},{2,0},{1,5},{5,9},... | collective-permute-start | bytes 786440 | tf_op jit(solution)/shard_map/ppermute | solution.py:624
  73.2 40.5 %collective-permute-start.11 = (bf16[64,2048]{1,0:T(8,128)(2,1)S(1)}, bf16[64,2048]{1,0:T(8,128)(2,1)S(1)}, u32[]{:S(2)}, u32[]{:S(2)}) collective-permute-start(bf16[64,2048]{1,0:T(8,128)(2,1)S(1)} %collective-permute-done.9.refs_2_), channel_id=1, source_target_pairs={{0,2},{4,0},{8,4},{12,8},{14,12},{10,14},{6,10},{2,6},{1,3},{5,1},... | collective-permute-start | bytes 786440 | tf_op jit(solution)/shard_map/ppermute | solution.py:624
  93.4 31.7 %collective-permute-start.18 = (bf16[64,2048]{1,0:T(8,128)(2,1)S(1)}, bf16[64,2048]{1,0:T(8,128)(2,1)S(1)}, u32[]{:S(2)}, u32[]{:S(2)}) collective-permute-start(bf16[64,2048]{1,0:T(8,128)(2,1)S(1)} %collective-permute-done.14.refs_1_), channel_id=1, source_target_pairs={{0,4},{4,8},{8,12},{12,14},{14,10},{10,6},{6,2},{2,0},{1,5},{5,9},... | collective-permute-start | bytes 786440 | tf_op jit(solution)/shard_map/ppermute | solution.py:624
  93.5 31.7 %collective-permute-start.19 = (bf16[64,2048]{1,0:T(8,128)(2,1)S(1)}, bf16[64,2048]{1,0:T(8,128)(2,1)S(1)}, u32[]{:S(2)}, u32[]{:S(2)}) collective-permute-start(bf16[64,2048]{1,0:T(8,128)(2,1)S(1)} %collective-permute-done.15.refs_2_), channel_id=1, source_target_pairs={{0,2},{4,0},{8,4},{12,8},{14,12},{10,14},{6,10},{2,6},{1,3},{5,1},... | collective-permute-start | bytes 786440 | tf_op jit(solution)/shard_map/ppermute | solution.py:624
  113.7 30.6 %collective-permute-start.17 = (bf16[64,2048]{1,0:T(8,128)(2,1)S(1)}, bf16[64,2048]{1,0:T(8,128)(2,1)S(1)}, u32[]{:S(2)}, u32[]{:S(2)}) collective-permute-start(bf16[64,2048]{1,0:T(8,128)(2,1)S(1)} %collective-permute-done.10.refs_1_), channel_id=1, source_target_pairs={{0,4},{4,8},{8,12},{12,14},{14,10},{10,6},{6,2},{2,0},{1,5},{5,9},... | collective-permute-start | bytes 786440 | tf_op jit(solution)/shard_map/ppermute | solution.py:624
  113.8 20.8 %collective-permute-start.20 = (bf16[64,2048]{1,0:T(8,128)(2,1)S(1)}, bf16[64,2048]{1,0:T(8,128)(2,1)S(1)}, u32[]{:S(2)}, u32[]{:S(2)}) collective-permute-start(bf16[64,2048]{1,0:T(8,128)(2,1)S(1)} %collective-permute-done.11.refs_2_), channel_id=1, source_target_pairs={{0,2},{4,0},{8,4},{12,8},{14,12},{10,14},{6,10},{2,6},{1,3},{5,1},... | collective-permute-start | bytes 786440 | tf_op jit(solution)/shard_map/ppermute | solution.py:624
where the time goes:
time: 154 us
  Pallas kernels  120 us (78%)
  starting transfers between devices  21.7 us (14%)
  waiting for transfers between devices  10.7 us (7%)
    pallas_call x4, Pallas kernels, attend_later(): pl.pallas_call(lambda *refs: later_kernel(places, *refs), out_shape=jax.S...  55.1 us
    pallas_call x1, Pallas kernels, attend_first(): pl.pallas_call(lambda *refs: first_kernel(kv_offsets, places, *refs), out...  31.8 us
    ppermute x21, starting transfers between devices, shift(): return lax.ppermute(block, 'replica', pairs)  21.7 us
    pallas_call x2, Pallas kernels, attend_last(): pl.pallas_call(lambda *refs: last_kernel(before, places, *refs), out_shap...  19.1 us
    pallas_call x1, Pallas kernels, attend_local(): pl.pallas_call(local_kernel, out_shape=jax.ShapeDtypeStruct((2 * SLOTS, S...  12.3 us
    ppermute x21, waiting for transfers between devices, shift(): return lax.ppermute(block, 'replica', pairs)  10.7 us
  transfers between devices with their start and end apart: 21, of which 5 were waited for; matrix products, arithmetic and copies ran while one was open for 0% of the time, Pallas kernels for 71%

commit v1 on v0

--- a/solution.py
+++ b/solution.py
@@ -673,13 +673,17 @@
         (shift(after(first[3][0], results[-1]), 1), farthest, 0),
         (shift(after(first[3][1], results[-1]), -1), farthest, half),
     ]
-    attend(3, first)
+
+    def attend_and_store(done, pieces, attention):
+        places = [[piece[1:] for piece in its_pieces] for its_pieces in before[done]]
+        return attend_last(
+            meta, places, results[done], pieces, ordered_keys, wide_values, attention
+        )
+
+    attention = attend_and_store(slice(0, 3), wave(3, first), attention)
     attend(3, second)
-    before = [[piece[1:] for piece in pieces] for pieces in before]
-    attention = attend_last(
-        meta, before, results, last[1:], ordered_keys, wide_values, attention
-    )
-    attention = attend_last(meta, [], [], last[:1], ordered_keys, wide_values, attention)
+    attention = attend_and_store(slice(3, 4), last[1:], attention)
+    attention = attend_and_store(slice(0, 0), last[:1], attention)
     return (attention, cache_keys, cache_values)
 
 

time: 154 us -> 153 us (level)
  the two profiles are of different devices: /device:TPU:0 before, /device:TPU:28 now
where the time goes in v1:
time: 153 us
  Pallas kernels  121 us (79%)
  starting transfers between devices  22.1 us (14%)
  waiting for transfers between devices  7.88 us (5%)
    pallas_call x3, Pallas kernels, attend_later(): pl.pallas_call(lambda *refs: later_kernel(places, *refs), out_shape=jax.S...  40.9 us
    pallas_call x1, Pallas kernels, attend_first(): pl.pallas_call(lambda *refs: first_kernel(kv_offsets, places, *refs), out...  36.6 us
    pallas_call x3, Pallas kernels, attend_last(): pl.pallas_call(lambda *refs: last_kernel(before, places, *refs), out_shap...  29.7 us
    ppermute x21, starting transfers between devices, shift(): return lax.ppermute(block, 'replica', pairs)  22.1 us
    pallas_call x1, Pallas kernels, attend_local(): pl.pallas_call(local_kernel, out_shape=jax.ShapeDtypeStruct((2 * SLOTS, S...  12.3 us
    ppermute x21, waiting for transfers between devices, shift(): return lax.ppermute(block, 'replica', pairs)  7.88 us
  transfers between devices with their start and end apart: 21, of which 5 were waited for; matrix products, arithmetic and copies ran while one was open for 0% of the time, Pallas kernels for 72%

profile of v1, /device:TPU:28, one launch (start us, length us, event | category | flops | bytes accessed | tf_op | source)
XLA Modules:
  0.0 152.6 jit_solution(18172704917978163356)
XLA Ops:
  0.6 0.0 copy-start.3
  0.6 0.0 copy-start.2
  0.7 0.0 copy-start.1
  0.7 0.0 copy-start.4
  0.7 0.0 copy-start.5
  0.7 0.0 copy-start
  0.7 1.6 %shard_map.85 = bf16[256,256]{1,0:T(8,128)(2,1)} custom-call(bf16[256,256]{1,0:T(8,128)(2,1)} %refs_1_.1, bf16[256,256]{1,0:T(8,128)(2,1)} %refs_2_.1), custom_call_target="tpu_custom_call" | custom-call | flops 1150000000 | tf_op jit(solution)/shard_map/pallas_call | solution.py:52
  2.3 0.5 collective-permute-start.3
  2.8 1.6 %collective-permute-start.2 = (bf16[256,256]{1,0:T(8,128)(2,1)}, bf16[256,256]{1,0:T(8,128)(2,1)S(1)}, u32[]{:S(2)}, u32[]{:S(2)}) collective-permute-start(bf16[256,256]{1,0:T(8,128)(2,1)} %shard_map.85), channel_id=1, source_target_pairs={{0,4},{4,8},{8,12},{12,14},{14,10},{10,6},{6,2},{2,0},{1,5},{5,9},... | collective-permute-start | bytes 393224 | tf_op jit(solution)/shard_map/ppermute | solution.py:624
  4.4 0.0 copy-done.1
  4.4 0.1 shard_map.86
  4.5 1.5 %collective-permute-start = (bf16[64,2048]{1,0:T(8,128)(2,1)S(1)}, bf16[64,2048]{1,0:T(8,128)(2,1)S(1)}, u32[]{:S(2)}, u32[]{:S(2)}) collective-permute-start(bf16[64,2048]{1,0:T(8,128)(2,1)S(1)} %get-tuple-element.63), channel_id=1, source_target_pairs={{0,4},{4,8},{8,12},{12,14},{14,10},{10,6},{6,2},{2,0},{1,5},{5,9},... | collective-permute-start | bytes 786440 | tf_op jit(solution)/shard_map/ppermute | solution.py:624
  6.0 0.5 collective-permute-start.1
  6.6 0.0 copy-done.4
  6.6 0.0 copy-done.5
  6.6 0.0 copy-done
  6.6 1.4 collective-permute-done.3.refs_4_
  8.0 1.5 collective-permute-done.2.refs_3_
  9.5 1.6 %collective-permute-start.4 = (bf16[256,256]{1,0:T(8,128)(2,1)S(1)}, bf16[256,256]{1,0:T(8,128)(2,1)S(1)}, u32[]{:S(2)}, u32[]{:S(2)}) collective-permute-start(bf16[256,256]{1,0:T(8,128)(2,1)S(1)} %collective-permute-done.2.refs_3_), channel_id=1, source_target_pairs={{0,4},{4,8},{8,12},{12,14},{14,10},{10,6},{6,2},{2,0},{1,5},{5,9},... | collective-permute-start | bytes 393224 | tf_op jit(solution)/shard_map/ppermute | solution.py:624
  11.1 0.4 collective-permute-start.5
  11.5 12.3 %shard_map.87.refs_14_ = bf16[4,64,2048]{2,1,0:T(8,128)(2,1)S(1)} custom-call(s32[8]{0:T(128)S(1)} %copy-done, bf16[256,2048]{1,0:T(8,128)(2,1)S(1)} %copy-done.1, bf16[256,256]{1,0:T(8,128)(2,1)S(1)} %copy-done.2, bf16[256,256]{1,0:T(8,128)(2,1)S(1)} %copy-done.3), custom_call_target="tpu_custom_call" | custom-call | flops 4024999936 | tf_op jit(solution)/shard_map/pallas_call | solution.py:339
  23.8 0.0 collective-permute-done.4.refs_5_
  23.8 0.0 collective-permute-done.5.refs_6_
  23.8 0.1 collective-permute-start.6
  23.9 2.0 %collective-permute-start.7 = (bf16[256,256]{1,0:T(8,128)(2,1)S(1)}, bf16[256,256]{1,0:T(8,128)(2,1)S(1)}, u32[]{:S(2)}, u32[]{:S(2)}) collective-permute-start(bf16[256,256]{1,0:T(8,128)(2,1)S(1)} %collective-permute-done.5.refs_6_), channel_id=1, source_target_pairs={{0,2},{4,0},{8,4},{12,8},{14,12},{10,14},{6,10},{2,6},{1,3},{5,1},... | collective-permute-start | bytes 393224 | tf_op jit(solution)/shard_map/ppermute | solution.py:624
  25.9 0.0 collective-permute-done.refs_10_
  25.9 0.0 collective-permute-done.1.refs_11_
  25.9 0.1 collective-permute-start.12
  26.0 2.0 %collective-permute-start.13 = (bf16[64,2048]{1,0:T(8,128)(2,1)S(1)}, bf16[64,2048]{1,0:T(8,128)(2,1)S(1)}, u32[]{:S(2)}, u32[]{:S(2)}) collective-permute-start(bf16[64,2048]{1,0:T(8,128)(2,1)S(1)} %get-tuple-element.63), channel_id=1, source_target_pairs={{0,2},{4,0},{8,4},{12,8},{14,12},{10,14},{6,10},{2,6},{1,3},{5,1},... | collective-permute-start | bytes 786440 | tf_op jit(solution)/shard_map/ppermute | solution.py:624
  28.0 0.2 add_reduce_fusion
  28.2 2.1 %collective-permute-done.6.refs_7_ = bf16[256,256]{1,0:T(8,128)(2,1)S(1)} collective-permute-done((bf16[256,256]{1,0:T(8,128)(2,1)S(1)}, bf16[256,256]{1,0:T(8,128)(2,1)S(1)}, u32[]{:S(2)}, u32[]{:S(2)}) %collective-permute-start.6) | collective-permute-done | bytes 131104 | tf_op jit(solution)/shard_map/ppermute | solution.py:624
  30.3 0.0 collective-permute-done.7.refs_8_
  30.3 0.5 collective-permute-start.16
  30.8 3.0 %collective-permute-start.8 = (bf16[64,2048]{1,0:T(8,128)(2,1)S(1)}, bf16[64,2048]{1,0:T(8,128)(2,1)S(1)}, u32[]{:S(2)}, u32[]{:S(2)}) collective-permute-start(bf16[64,2048]{1,0:T(8,128)(2,1)S(1)} %collective-permute-done.refs_10_), channel_id=1, source_target_pairs={{0,4},{4,8},{8,12},{12,14},{14,10},{10,6},{6,2},{2,0},{1,5},{5,9},... | collective-permute-start | bytes 786440 | tf_op jit(solution)/shard_map/ppermute | solution.py:624
  33.8 0.0 collective-permute-start.9
  33.8 2.1 %collective-permute-done.12.refs_12_ = bf16[64,2048]{1,0:T(8,128)(2,1)S(1)} collective-permute-done((bf16[64,2048]{1,0:T(8,128)(2,1)S(1)}, bf16[64,2048]{1,0:T(8,128)(2,1)S(1)}, u32[]{:S(2)}, u32[]{:S(2)}) %collective-permute-start.12) | collective-permute-done | bytes 262176 | tf_op jit(solution)/shard_map/ppermute | solution.py:624
  35.9 0.0 collective-permute-done.13.refs_13_
  35.9 0.7 collective-permute-start.14
  36.6 1.3 collective-permute-start.15
  37.9 0.8 collective-permute-done.16.refs_9_
  38.7 0.1 broadcast_in_dim.32.refs_0_
  38.8 36.6 %shard_map.88 = (bf16[1024,256]{1,0:T(8,128)(2,1)}, bf16[1024,256]{1,0:T(8,128)(2,1)}, bf16[1024,256]{1,0:T(8,128)(2,1)S(1)}, bf16[1024,512]{1,0:T(8,128)(2,1)S(...) custom-call(s32[8,128]{1,0:T(8,128)S(1)} %broadcast_in_dim.32.refs_0_, bf16[256,256]{1,0:T(8,128)(2,1)S(1)} %copy-done.2, ...), custom_call_target="tpu_custom_call" | custom-call | flops 8280000000 | tf_op jit(solution)/shard_map/pallas_call | solution.py:429
  75.4 0.0 collective-permute-done.8.refs_1_
  75.4 0.0 collective-permute-done.9.refs_2_
  75.4 0.1 collective-permute-start.10
  75.5 2.0 %collective-permute-start.11 = (bf16[64,2048]{1,0:T(8,128)(2,1)S(1)}, bf16[64,2048]{1,0:T(8,128)(2,1)S(1)}, u32[]{:S(2)}, u32[]{:S(2)}) collective-permute-start(bf16[64,2048]{1,0:T(8,128)(2,1)S(1)} %collective-permute-done.9.refs_2_), channel_id=1, source_target_pairs={{0,2},{4,0},{8,4},{12,8},{14,12},{10,14},{6,10},{2,6},{1,3},{5,1},... | collective-permute-start | bytes 786440 | tf_op jit(solution)/shard_map/ppermute | solution.py:624
  77.5 15.8 %shard_map.90.refs_2_ = bf16[2,64,2048]{2,1,0:T(8,128)(2,1)S(1)} custom-call(s32[8,128]{1,0:T(8,128)S(1)} %broadcast_in_dim.32.refs_0_, bf16[64,2048]{1,0:T(8,128)(2,1)S(1)} %collective-permute-done.8.refs_1_, bf16[64,2048]{1,0:T(8,128)(2,1)S(1)} %collective-permute-done.9.refs_2_, bf16[1024,256]{1,0:T(8,128)(2,1)S(1)} %get-tuple-element.70.refs_3_.refs_6_.refs_2_, ...), custom_call_target="tpu_custom_call" | custom-call | flops 4140000000 | tf_op jit(solution)/shard_map/pallas_call | solution.py:467
  93.3 0.0 collective-permute-done.14.refs_1_
  93.3 0.0 collective-permute-done.15.refs_2_
  93.3 0.1 collective-permute-start.18
  93.4 2.0 %collective-permute-start.19 = (bf16[64,2048]{1,0:T(8,128)(2,1)S(1)}, bf16[64,2048]{1,0:T(8,128)(2,1)S(1)}, u32[]{:S(2)}, u32[]{:S(2)}) collective-permute-start(bf16[64,2048]{1,0:T(8,128)(2,1)S(1)} %collective-permute-done.15.refs_2_), channel_id=1, source_target_pairs={{0,2},{4,0},{8,4},{12,8},{14,12},{10,14},{6,10},{2,6},{1,3},{5,1},... | collective-permute-start | bytes 786440 | tf_op jit(solution)/shard_map/ppermute | solution.py:624
  95.4 15.8 %shard_map.89.refs_3_ = bf16[2,64,2048]{2,1,0:T(8,128)(2,1)S(1)} custom-call(s32[8,128]{1,0:T(8,128)S(1)} %broadcast_in_dim.32.refs_0_, bf16[64,2048]{1,0:T(8,128)(2,1)S(1)} %collective-permute-done.14.refs_1_, bf16[64,2048]{1,0:T(8,128)(2,1)S(1)} %collective-permute-done.15.refs_2_, bf16[1024,256]{1,0:T(8,128)(2,1)S(1)} %get-tuple-element.70.refs_3_.refs_6_.refs_2_, ...), custom_call_target="tpu_custom_call" | custom-call | flops 4140000000 | tf_op jit(solution)/shard_map/pallas_call | solution.py:467
  111.2 0.0 collective-permute-done.10.refs_4_
  111.2 0.0 collective-permute-done.11.refs_5_
  111.2 0.1 collective-permute-start.17
  111.3 2.0 %collective-permute-start.20 = (bf16[64,2048]{1,0:T(8,128)(2,1)S(1)}, bf16[64,2048]{1,0:T(8,128)(2,1)S(1)}, u32[]{:S(2)}, u32[]{:S(2)}) collective-permute-start(bf16[64,2048]{1,0:T(8,128)(2,1)S(1)} %collective-permute-done.11.refs_5_), channel_id=1, source_target_pairs={{0,2},{4,0},{8,4},{12,8},{14,12},{10,14},{6,10},{2,6},{1,3},{5,1},... | collective-permute-start | bytes 786440 | tf_op jit(solution)/shard_map/ppermute | solution.py:624
  113.3 10.8 %shard_map.92.refs_5_ = bf16[1024,2048]{1,0:T(8,128)(2,1)} custom-call(s32[8,128]{1,0:T(8,128)S(1)} %broadcast_in_dim.32.refs_0_, bf16[4,64,2048]{2,1,0:T(8,128)(2,1)S(1)} %get-tuple-element.79.refs_1_, bf16[2,64,2048]{2,1,0:T(8,128)(2,1)S(1)} %shard_map.90.refs_2_, bf16[2,64,2048]{2,1,0:T(8,128)(2,1)S(1)} %shard_map.89.refs_3_, ...), custom_call_target="tpu_custom_call", output_to_operand_aliasing={{}: (8, {})} | custom-call | flops 2875000064 | tf_op jit(solution)/shard_map/pallas_call | solution.py:512
  124.1 0.0 collective-permute-done.18.refs_1_
  124.1 0.0 collective-permute-done.19.refs_2_
  124.1 9.4 %shard_map.91.refs_1_ = bf16[2,64,2048]{2,1,0:T(8,128)(2,1)S(1)} custom-call(s32[8,128]{1,0:T(8,128)S(1)} %broadcast_in_dim.32.refs_0_, bf16[64,2048]{1,0:T(8,128)(2,1)S(1)} %collective-permute-done.18.refs_1_, bf16[64,2048]{1,0:T(8,128)(2,1)S(1)} %collective-permute-done.19.refs_2_, bf16[1024,256]{1,0:T(8,128)(2,1)S(1)} %get-tuple-element.70.refs_3_.refs_6_.refs_2_, ...), custom_call_target="tpu_custom_call" | custom-call | flops 4140000000 | tf_op jit(solution)/shard_map/pallas_call | solution.py:467
  133.5 0.0 collective-permute-done.20.refs_2_
  133.5 9.4 %shard_map.93.refs_4_ = bf16[1024,2048]{1,0:T(8,128)(2,1)} custom-call(s32[8,128]{1,0:T(8,128)S(1)} %broadcast_in_dim.32.refs_0_, bf16[2,64,2048]{2,1,0:T(8,128)(2,1)S(1)} %shard_map.91.refs_1_, bf16[64,2048]{1,0:T(8,128)(2,1)S(1)} %collective-permute-done.20.refs_2_, ...), custom_call_target="tpu_custom_call", output_to_operand_aliasing={{}: (5, {})} | custom-call | flops 2875000064 | tf_op jit(solution)/shard_map/pallas_call | solution.py:512
  143.0 0.0 collective-permute-done.17.refs_1_
  143.0 9.4 %shard_map.94 = bf16[1024,2048]{1,0:T(8,128)(2,1)} custom-call(s32[8,128]{1,0:T(8,128)S(1)} %broadcast_in_dim.32.refs_0_, bf16[64,2048]{1,0:T(8,128)(2,1)S(1)} %collective-permute-done.17.refs_1_, bf16[1024,256]{1,0:T(8,128)(2,1)S(1)} %get-tuple-element.70.refs_3_.refs_6_.refs_2_, ...), custom_call_target="tpu_custom_call", output_to_operand_aliasing={{}: (4, {})} | custom-call | flops 2875000064 | tf_op jit(solution)/shard_map/pallas_call | solution.py:512
  (7 shorter events, 0.0 us)
Async XLA Ops:
  0.6 10.9 %copy-start.3 = (bf16[256,256]{1,0:T(8,128)(2,1)S(1)}, bf16[256,256]{1,0:T(8,128)(2,1)}, u32[]{:S(2)}) copy-start(bf16[256,256]{1,0:T(8,128)(2,1)} %refs_2_.1) | copy-start | bytes 393220
  0.6 10.9 %copy-start.2 = (bf16[256,256]{1,0:T(8,128)(2,1)S(1)}, bf16[256,256]{1,0:T(8,128)(2,1)}, u32[]{:S(2)}) copy-start(bf16[256,256]{1,0:T(8,128)(2,1)} %refs_1_.1) | copy-start | bytes 393220
  0.7 3.8 %copy-start.1 = (bf16[256,2048]{1,0:T(8,128)(2,1)S(1)}, bf16[256,2048]{1,0:T(8,128)(2,1)}, u32[]{:S(2)}) copy-start(bf16[256,2048]{1,0:T(8,128)(2,1)} %q_ref.1) | copy-start | bytes 3145732
  0.7 5.9 %copy-start.4 = (s32[8,2]{0,1:T(2,128)S(1)}, s32[8,2]{0,1:T(2,128)}, u32[]{:S(2)}) copy-start(s32[8,2]{0,1:T(2,128)} %param.10) | copy-start | bytes 196
  0.7 5.9 %copy-start.5 = (s32[8,2]{0,1:T(2,128)S(1)}, s32[8,2]{0,1:T(2,128)}, u32[]{:S(2)}) copy-start(s32[8,2]{0,1:T(2,128)} %param.11) | copy-start | bytes 196
  0.7 5.9 %copy-start = (s32[8]{0:T(128)S(1)}, s32[8]{0:T(128)}, u32[]{:S(2)}) copy-start(s32[8]{0:T(128)} %length_ref.1) | copy-start | bytes 100
  2.3 5.7 %collective-permute-start.3 = (bf16[256,256]{1,0:T(8,128)(2,1)}, bf16[256,256]{1,0:T(8,128)(2,1)S(1)}, u32[]{:S(2)}, u32[]{:S(2)}) collective-permute-start(bf16[256,256]{1,0:T(8,128)(2,1)} %shard_map.85), channel_id=1, source_target_pairs={{0,2},{4,0},{8,4},{12,8},{14,12},{10,14},{6,10},{2,6},{1,3},{5,1},... | collective-permute-start | bytes 393224 | tf_op jit(solution)/shard_map/ppermute | solution.py:624
  2.8 6.6 %collective-permute-start.2 = (bf16[256,256]{1,0:T(8,128)(2,1)}, bf16[256,256]{1,0:T(8,128)(2,1)S(1)}, u32[]{:S(2)}, u32[]{:S(2)}) collective-permute-start(bf16[256,256]{1,0:T(8,128)(2,1)} %shard_map.85), channel_id=1, source_target_pairs={{0,4},{4,8},{8,12},{12,14},{14,10},{10,6},{6,2},{2,0},{1,5},{5,9},... | collective-permute-start | bytes 393224 | tf_op jit(solution)/shard_map/ppermute | solution.py:624
  4.5 21.4 %collective-permute-start = (bf16[64,2048]{1,0:T(8,128)(2,1)S(1)}, bf16[64,2048]{1,0:T(8,128)(2,1)S(1)}, u32[]{:S(2)}, u32[]{:S(2)}) collective-permute-start(bf16[64,2048]{1,0:T(8,128)(2,1)S(1)} %get-tuple-element.63), channel_id=1, source_target_pairs={{0,4},{4,8},{8,12},{12,14},{14,10},{10,6},{6,2},{2,0},{1,5},{5,9},... | collective-permute-start | bytes 786440 | tf_op jit(solution)/shard_map/ppermute | solution.py:624
  6.0 19.9 %collective-permute-start.1 = (bf16[64,2048]{1,0:T(8,128)(2,1)S(1)}, bf16[64,2048]{1,0:T(8,128)(2,1)S(1)}, u32[]{:S(2)}, u32[]{:S(2)}) collective-permute-start(bf16[64,2048]{1,0:T(8,128)(2,1)S(1)} %get-tuple-element.62), channel_id=1, source_target_pairs={{0,2},{4,0},{8,4},{12,8},{14,12},{10,14},{6,10},{2,6},{1,3},{5,1},... | collective-permute-start | bytes 786440 | tf_op jit(solution)/shard_map/ppermute | solution.py:624
  9.5 14.3 %collective-permute-start.4 = (bf16[256,256]{1,0:T(8,128)(2,1)S(1)}, bf16[256,256]{1,0:T(8,128)(2,1)S(1)}, u32[]{:S(2)}, u32[]{:S(2)}) collective-permute-start(bf16[256,256]{1,0:T(8,128)(2,1)S(1)} %collective-permute-done.2.refs_3_), channel_id=1, source_target_pairs={{0,4},{4,8},{8,12},{12,14},{14,10},{10,6},{6,2},{2,0},{1,5},{5,9},... | collective-permute-start | bytes 393224 | tf_op jit(solution)/shard_map/ppermute | solution.py:624
  11.1 12.7 %collective-permute-start.5 = (bf16[256,256]{1,0:T(8,128)(2,1)S(1)}, bf16[256,256]{1,0:T(8,128)(2,1)S(1)}, u32[]{:S(2)}, u32[]{:S(2)}) collective-permute-start(bf16[256,256]{1,0:T(8,128)(2,1)S(1)} %collective-permute-done.3.refs_4_), channel_id=1, source_target_pairs={{0,2},{4,0},{8,4},{12,8},{14,12},{10,14},{6,10},{2,6},{1,3},{5,1},... | collective-permute-start | bytes 393224 | tf_op jit(solution)/shard_map/ppermute | solution.py:624
  23.8 6.5 %collective-permute-start.6 = (bf16[256,256]{1,0:T(8,128)(2,1)S(1)}, bf16[256,256]{1,0:T(8,128)(2,1)S(1)}, u32[]{:S(2)}, u32[]{:S(2)}) collective-permute-start(bf16[256,256]{1,0:T(8,128)(2,1)S(1)} %collective-permute-done.4.refs_5_), channel_id=1, source_target_pairs={{0,4},{4,8},{8,12},{12,14},{14,10},{10,6},{6,2},{2,0},{1,5},{5,9},... | collective-permute-start | bytes 393224 | tf_op jit(solution)/shard_map/ppermute | solution.py:624
  23.9 6.4 %collective-permute-start.7 = (bf16[256,256]{1,0:T(8,128)(2,1)S(1)}, bf16[256,256]{1,0:T(8,128)(2,1)S(1)}, u32[]{:S(2)}, u32[]{:S(2)}) collective-permute-start(bf16[256,256]{1,0:T(8,128)(2,1)S(1)} %collective-permute-done.5.refs_6_), channel_id=1, source_target_pairs={{0,2},{4,0},{8,4},{12,8},{14,12},{10,14},{6,10},{2,6},{1,3},{5,1},... | collective-permute-start | bytes 393224 | tf_op jit(solution)/shard_map/ppermute | solution.py:624
  25.9 10.0 %collective-permute-start.12 = (bf16[64,2048]{1,0:T(8,128)(2,1)S(1)}, bf16[64,2048]{1,0:T(8,128)(2,1)S(1)}, u32[]{:S(2)}, u32[]{:S(2)}) collective-permute-start(bf16[64,2048]{1,0:T(8,128)(2,1)S(1)} %get-tuple-element.62), channel_id=1, source_target_pairs={{0,4},{4,8},{8,12},{12,14},{14,10},{10,6},{6,2},{2,0},{1,5},{5,9},... | collective-permute-start | bytes 786440 | tf_op jit(solution)/shard_map/ppermute | solution.py:624
  26.0 9.9 %collective-permute-start.13 = (bf16[64,2048]{1,0:T(8,128)(2,1)S(1)}, bf16[64,2048]{1,0:T(8,128)(2,1)S(1)}, u32[]{:S(2)}, u32[]{:S(2)}) collective-permute-start(bf16[64,2048]{1,0:T(8,128)(2,1)S(1)} %get-tuple-element.63), channel_id=1, source_target_pairs={{0,2},{4,0},{8,4},{12,8},{14,12},{10,14},{6,10},{2,6},{1,3},{5,1},... | collective-permute-start | bytes 786440 | tf_op jit(solution)/shard_map/ppermute | solution.py:624
  30.3 8.4 %collective-permute-start.16 = (bf16[256,256]{1,0:T(8,128)(2,1)S(1)}, bf16[256,256]{1,0:T(8,128)(2,1)S(1)}, u32[]{:S(2)}, u32[]{:S(2)}) collective-permute-start(bf16[256,256]{1,0:T(8,128)(2,1)S(1)} %collective-permute-done.6.refs_7_), channel_id=1, source_target_pairs={{0,4},{4,8},{8,12},{12,14},{14,10},{10,6},{6,2},{2,0},{1,5},{5,9},... | collective-permute-start | bytes 393224 | tf_op jit(solution)/shard_map/ppermute | solution.py:624
  30.8 44.6 %collective-permute-start.8 = (bf16[64,2048]{1,0:T(8,128)(2,1)S(1)}, bf16[64,2048]{1,0:T(8,128)(2,1)S(1)}, u32[]{:S(2)}, u32[]{:S(2)}) collective-permute-start(bf16[64,2048]{1,0:T(8,128)(2,1)S(1)} %collective-permute-done.refs_10_), channel_id=1, source_target_pairs={{0,4},{4,8},{8,12},{12,14},{14,10},{10,6},{6,2},{2,0},{1,5},{5,9},... | collective-permute-start | bytes 786440 | tf_op jit(solution)/shard_map/ppermute | solution.py:624
  33.8 41.6 %collective-permute-start.9 = (bf16[64,2048]{1,0:T(8,128)(2,1)S(1)}, bf16[64,2048]{1,0:T(8,128)(2,1)S(1)}, u32[]{:S(2)}, u32[]{:S(2)}) collective-permute-start(bf16[64,2048]{1,0:T(8,128)(2,1)S(1)} %collective-permute-done.1.refs_11_), channel_id=1, source_target_pairs={{0,2},{4,0},{8,4},{12,8},{14,12},{10,14},{6,10},{2,6},{1,3},{5,1},... | collective-permute-start | bytes 786440 | tf_op jit(solution)/shard_map/ppermute | solution.py:624
  35.9 57.4 %collective-permute-start.14 = (bf16[64,2048]{1,0:T(8,128)(2,1)S(1)}, bf16[64,2048]{1,0:T(8,128)(2,1)S(1)}, u32[]{:S(2)}, u32[]{:S(2)}) collective-permute-start(bf16[64,2048]{1,0:T(8,128)(2,1)S(1)} %collective-permute-done.12.refs_12_), channel_id=1, source_target_pairs={{0,4},{4,8},{8,12},{12,14},{14,10},{10,6},{6,2},{2,0},{1,5},{5,9},... | collective-permute-start | bytes 786440 | tf_op jit(solution)/shard_map/ppermute | solution.py:624
  36.6 56.7 %collective-permute-start.15 = (bf16[64,2048]{1,0:T(8,128)(2,1)S(1)}, bf16[64,2048]{1,0:T(8,128)(2,1)S(1)}, u32[]{:S(2)}, u32[]{:S(2)}) collective-permute-start(bf16[64,2048]{1,0:T(8,128)(2,1)S(1)} %collective-permute-done.13.refs_13_), channel_id=1, source_target_pairs={{0,2},{4,0},{8,4},{12,8},{14,12},{10,14},{6,10},{2,6},{1,3},{5,1},... | collective-permute-start | bytes 786440 | tf_op jit(solution)/shard_map/ppermute | solution.py:624
  75.4 35.8 %collective-permute-start.10 = (bf16[64,2048]{1,0:T(8,128)(2,1)S(1)}, bf16[64,2048]{1,0:T(8,128)(2,1)S(1)}, u32[]{:S(2)}, u32[]{:S(2)}) collective-permute-start(bf16[64,2048]{1,0:T(8,128)(2,1)S(1)} %collective-permute-done.8.refs_1_), channel_id=1, source_target_pairs={{0,4},{4,8},{8,12},{12,14},{14,10},{10,6},{6,2},{2,0},{1,5},{5,9},... | collective-permute-start | bytes 786440 | tf_op jit(solution)/shard_map/ppermute | solution.py:624
  75.5 35.7 %collective-permute-start.11 = (bf16[64,2048]{1,0:T(8,128)(2,1)S(1)}, bf16[64,2048]{1,0:T(8,128)(2,1)S(1)}, u32[]{:S(2)}, u32[]{:S(2)}) collective-permute-start(bf16[64,2048]{1,0:T(8,128)(2,1)S(1)} %collective-permute-done.9.refs_2_), channel_id=1, source_target_pairs={{0,2},{4,0},{8,4},{12,8},{14,12},{10,14},{6,10},{2,6},{1,3},{5,1},... | collective-permute-start | bytes 786440 | tf_op jit(solution)/shard_map/ppermute | solution.py:624
  93.3 30.8 %collective-permute-start.18 = (bf16[64,2048]{1,0:T(8,128)(2,1)S(1)}, bf16[64,2048]{1,0:T(8,128)(2,1)S(1)}, u32[]{:S(2)}, u32[]{:S(2)}) collective-permute-start(bf16[64,2048]{1,0:T(8,128)(2,1)S(1)} %collective-permute-done.14.refs_1_), channel_id=1, source_target_pairs={{0,4},{4,8},{8,12},{12,14},{14,10},{10,6},{6,2},{2,0},{1,5},{5,9},... | collective-permute-start | bytes 786440 | tf_op jit(solution)/shard_map/ppermute | solution.py:624
  93.4 30.7 %collective-permute-start.19 = (bf16[64,2048]{1,0:T(8,128)(2,1)S(1)}, bf16[64,2048]{1,0:T(8,128)(2,1)S(1)}, u32[]{:S(2)}, u32[]{:S(2)}) collective-permute-start(bf16[64,2048]{1,0:T(8,128)(2,1)S(1)} %collective-permute-done.15.refs_2_), channel_id=1, source_target_pairs={{0,2},{4,0},{8,4},{12,8},{14,12},{10,14},{6,10},{2,6},{1,3},{5,1},... | collective-permute-start | bytes 786440 | tf_op jit(solution)/shard_map/ppermute | solution.py:624
  111.2 31.8 %collective-permute-start.17 = (bf16[64,2048]{1,0:T(8,128)(2,1)S(1)}, bf16[64,2048]{1,0:T(8,128)(2,1)S(1)}, u32[]{:S(2)}, u32[]{:S(2)}) collective-permute-start(bf16[64,2048]{1,0:T(8,128)(2,1)S(1)} %collective-permute-done.10.refs_4_), channel_id=1, source_target_pairs={{0,4},{4,8},{8,12},{12,14},{14,10},{10,6},{6,2},{2,0},{1,5},{5,9},... | collective-permute-start | bytes 786440 | tf_op jit(solution)/shard_map/ppermute | solution.py:624
  111.3 22.2 %collective-permute-start.20 = (bf16[64,2048]{1,0:T(8,128)(2,1)S(1)}, bf16[64,2048]{1,0:T(8,128)(2,1)S(1)}, u32[]{:S(2)}, u32[]{:S(2)}) collective-permute-start(bf16[64,2048]{1,0:T(8,128)(2,1)S(1)} %collective-permute-done.11.refs_5_), channel_id=1, source_target_pairs={{0,2},{4,0},{8,4},{12,8},{14,12},{10,14},{6,10},{2,6},{1,3},{5,1},... | collective-permute-start | bytes 786440 | tf_op jit(solution)/shard_map/ppermute | solution.py:624

commit v2 on v1

--- a/solution.py
+++ b/solution.py
@@ -14,7 +14,7 @@
 LANES = 128
 MAXC = 8
 BLOCK = 4
-PART = 2
+PART = 1
 LOG2E = 1.0 / math.log(2.0)
 VMEM_BYTES = 40 * 1024 * 1024
 MOST_VMEM_BYTES = 60 * 1024 * 1024

time: 153 us -> 154 us (level)
  the two profiles are of different devices: /device:TPU:28 before, /device:TPU:16 now
where the time goes in v2:
time: 154 us; the launch traced here: 153 us
  Pallas kernels  121 us (79%)
  starting transfers between devices  24.4 us (16%)
  waiting for transfers between devices  5.92 us (4%)
    pallas_call x3, Pallas kernels, attend_last(): pl.pallas_call(lambda *refs: last_kernel(before, places, *refs), out_shap...  37 us
    pallas_call x3, Pallas kernels, attend_later(): pl.pallas_call(lambda *refs: later_kernel(places, *refs), out_shape=jax.S...  35.8 us
    pallas_call x1, Pallas kernels, attend_first(): pl.pallas_call(lambda *refs: first_kernel(kv_offsets, places, *refs), out...  34.4 us
    ppermute x21, starting transfers between devices, shift(): return lax.ppermute(block, 'replica', pairs)  24.4 us
    pallas_call x1, Pallas kernels, attend_local(): pl.pallas_call(local_kernel, out_shape=jax.ShapeDtypeStruct((2 * SLOTS, S...  12.2 us
    ppermute x21, waiting for transfers between devices, shift(): return lax.ppermute(block, 'replica', pairs)  5.92 us
  transfers between devices with their start and end apart: 21, of which 5 were waited for; matrix products, arithmetic and copies ran while one was open for 0% of the time, Pallas kernels for 74%

profile of v2, /device:TPU:16, one launch (start us, length us, event | category | flops | bytes accessed | tf_op | source)
XLA Modules:
  0.0 152.8 jit_solution(15548782526012180649)
XLA Ops:
  0.6 0.0 copy-start.3
  0.6 0.0 copy-start.2
  0.7 0.0 copy-start.1
  0.7 0.0 copy-start.4
  0.7 0.0 copy-start.5
  0.7 0.0 copy-start
  0.7 1.6 %shard_map.85 = bf16[256,256]{1,0:T(8,128)(2,1)} custom-call(bf16[256,256]{1,0:T(8,128)(2,1)} %refs_1_.1, bf16[256,256]{1,0:T(8,128)(2,1)} %refs_2_.1), custom_call_target="tpu_custom_call" | custom-call | flops 1150000000 | tf_op jit(solution)/shard_map/pallas_call | solution.py:52
  2.3 0.5 collective-permute-start.3
  2.8 1.6 %collective-permute-start.2 = (bf16[256,256]{1,0:T(8,128)(2,1)}, bf16[256,256]{1,0:T(8,128)(2,1)S(1)}, u32[]{:S(2)}, u32[]{:S(2)}) collective-permute-start(bf16[256,256]{1,0:T(8,128)(2,1)} %shard_map.85), channel_id=1, source_target_pairs={{0,4},{4,8},{8,12},{12,14},{14,10},{10,6},{6,2},{2,0},{1,5},{5,9},... | collective-permute-start | bytes 393224 | tf_op jit(solution)/shard_map/ppermute | solution.py:624
  4.4 0.0 copy-done.1
  4.4 0.1 shard_map.86
  4.5 1.6 %collective-permute-start = (bf16[64,2048]{1,0:T(8,128)(2,1)S(1)}, bf16[64,2048]{1,0:T(8,128)(2,1)S(1)}, u32[]{:S(2)}, u32[]{:S(2)}) collective-permute-start(bf16[64,2048]{1,0:T(8,128)(2,1)S(1)} %get-tuple-element.63), channel_id=1, source_target_pairs={{0,4},{4,8},{8,12},{12,14},{14,10},{10,6},{6,2},{2,0},{1,5},{5,9},... | collective-permute-start | bytes 786440 | tf_op jit(solution)/shard_map/ppermute | solution.py:624
  6.1 0.4 collective-permute-start.1
  6.6 0.0 copy-done.4
  6.6 0.0 copy-done.5
  6.6 1.3 collective-permute-done.3.refs_4_
  7.9 1.6 %collective-permute-done.2.refs_3_ = bf16[256,256]{1,0:T(8,128)(2,1)S(1)} collective-permute-done((bf16[256,256]{1,0:T(8,128)(2,1)}, bf16[256,256]{1,0:T(8,128)(2,1)S(1)}, u32[]{:S(2)}, u32[]{:S(2)}) %collective-permute-start.2) | collective-permute-done | bytes 131104 | tf_op jit(solution)/shard_map/ppermute | solution.py:624
  9.5 1.6 %collective-permute-start.4 = (bf16[256,256]{1,0:T(8,128)(2,1)S(1)}, bf16[256,256]{1,0:T(8,128)(2,1)S(1)}, u32[]{:S(2)}, u32[]{:S(2)}) collective-permute-start(bf16[256,256]{1,0:T(8,128)(2,1)S(1)} %collective-permute-done.2.refs_3_), channel_id=1, source_target_pairs={{0,4},{4,8},{8,12},{12,14},{14,10},{10,6},{6,2},{2,0},{1,5},{5,9},... | collective-permute-start | bytes 393224 | tf_op jit(solution)/shard_map/ppermute | solution.py:624
  11.1 0.4 collective-permute-start.5
  11.5 0.0 copy-done.3
  11.5 12.2 %shard_map.87.refs_14_ = bf16[4,64,2048]{2,1,0:T(8,128)(2,1)S(1)} custom-call(s32[8]{0:T(128)S(1)} %copy-done, bf16[256,2048]{1,0:T(8,128)(2,1)S(1)} %copy-done.1, bf16[256,256]{1,0:T(8,128)(2,1)S(1)} %copy-done.2, bf16[256,256]{1,0:T(8,128)(2,1)S(1)} %copy-done.3), custom_call_target="tpu_custom_call" | custom-call | flops 4024999936 | tf_op jit(solution)/shard_map/pallas_call | solution.py:339
  23.7 0.0 collective-permute-done.4.refs_5_
  23.7 0.0 collective-permute-done.5.refs_6_
  23.7 0.1 collective-permute-start.6
  23.8 2.0 %collective-permute-start.7 = (bf16[256,256]{1,0:T(8,128)(2,1)S(1)}, bf16[256,256]{1,0:T(8,128)(2,1)S(1)}, u32[]{:S(2)}, u32[]{:S(2)}) collective-permute-start(bf16[256,256]{1,0:T(8,128)(2,1)S(1)} %collective-permute-done.5.refs_6_), channel_id=1, source_target_pairs={{0,2},{4,0},{8,4},{12,8},{14,12},{10,14},{6,10},{2,6},{1,3},{5,1},... | collective-permute-start | bytes 393224 | tf_op jit(solution)/shard_map/ppermute | solution.py:624
  25.8 0.0 collective-permute-done.refs_10_
  25.8 0.0 collective-permute-done.1.refs_11_
  25.8 1.2 collective-permute-start.12
  27.0 0.9 collective-permute-start.13
  27.9 0.2 add_reduce_fusion
  28.1 1.7 %collective-permute-done.6.refs_7_ = bf16[256,256]{1,0:T(8,128)(2,1)S(1)} collective-permute-done((bf16[256,256]{1,0:T(8,128)(2,1)S(1)}, bf16[256,256]{1,0:T(8,128)(2,1)S(1)}, u32[]{:S(2)}, u32[]{:S(2)}) %collective-permute-start.6) | collective-permute-done | bytes 131104 | tf_op jit(solution)/shard_map/ppermute | solution.py:624
  29.8 0.5 collective-permute-done.7.refs_8_
  30.3 3.0 %collective-permute-start.16 = (bf16[256,256]{1,0:T(8,128)(2,1)S(1)}, bf16[256,256]{1,0:T(8,128)(2,1)S(1)}, u32[]{:S(2)}, u32[]{:S(2)}) collective-permute-start(bf16[256,256]{1,0:T(8,128)(2,1)S(1)} %collective-permute-done.6.refs_7_), channel_id=1, source_target_pairs={{0,4},{4,8},{8,12},{12,14},{14,10},{10,6},{6,2},{2,0},{1,5},{5,9},... | collective-permute-start | bytes 393224 | tf_op jit(solution)/shard_map/ppermute | solution.py:624
  33.4 0.1 collective-permute-start.8
  33.4 2.0 %collective-permute-start.9 = (bf16[64,2048]{1,0:T(8,128)(2,1)S(1)}, bf16[64,2048]{1,0:T(8,128)(2,1)S(1)}, u32[]{:S(2)}, u32[]{:S(2)}) collective-permute-start(bf16[64,2048]{1,0:T(8,128)(2,1)S(1)} %collective-permute-done.1.refs_11_), channel_id=1, source_target_pairs={{0,2},{4,0},{8,4},{12,8},{14,12},{10,14},{6,10},{2,6},{1,3},{5,1},... | collective-permute-start | bytes 786440 | tf_op jit(solution)/shard_map/ppermute | solution.py:624
  35.4 0.0 collective-permute-done.12.refs_12_
  35.4 0.7 collective-permute-done.13.refs_13_
  36.2 2.8 %collective-permute-start.14 = (bf16[64,2048]{1,0:T(8,128)(2,1)S(1)}, bf16[64,2048]{1,0:T(8,128)(2,1)S(1)}, u32[]{:S(2)}, u32[]{:S(2)}) collective-permute-start(bf16[64,2048]{1,0:T(8,128)(2,1)S(1)} %collective-permute-done.12.refs_12_), channel_id=1, source_target_pairs={{0,4},{4,8},{8,12},{12,14},{14,10},{10,6},{6,2},{2,0},{1,5},{5,9},... | collective-permute-start | bytes 786440 | tf_op jit(solution)/shard_map/ppermute | solution.py:624
  39.0 0.0 collective-permute-start.15
  39.0 0.0 collective-permute-done.16.refs_9_
  39.0 0.1 broadcast_in_dim.32.refs_0_
  39.1 34.4 %shard_map.88 = (bf16[1024,256]{1,0:T(8,128)(2,1)}, bf16[1024,256]{1,0:T(8,128)(2,1)}, bf16[1024,256]{1,0:T(8,128)(2,1)S(1)}, bf16[1024,512]{1,0:T(8,128)(2,1)S(...) custom-call(s32[8,128]{1,0:T(8,128)S(1)} %broadcast_in_dim.32.refs_0_, bf16[256,256]{1,0:T(8,128)(2,1)S(1)} %copy-done.2, ...), custom_call_target="tpu_custom_call" | custom-call | flops 8280000000 | tf_op jit(solution)/shard_map/pallas_call | solution.py:429
  73.5 0.0 collective-permute-done.8.refs_1_
  73.5 0.0 collective-permute-done.9.refs_2_
  73.5 0.1 collective-permute-start.10
  73.6 2.0 %collective-permute-start.11 = (bf16[64,2048]{1,0:T(8,128)(2,1)S(1)}, bf16[64,2048]{1,0:T(8,128)(2,1)S(1)}, u32[]{:S(2)}, u32[]{:S(2)}) collective-permute-start(bf16[64,2048]{1,0:T(8,128)(2,1)S(1)} %collective-permute-done.9.refs_2_), channel_id=1, source_target_pairs={{0,2},{4,0},{8,4},{12,8},{14,12},{10,14},{6,10},{2,6},{1,3},{5,1},... | collective-permute-start | bytes 786440 | tf_op jit(solution)/shard_map/ppermute | solution.py:624
  75.6 6.5 %shard_map.90.refs_2_ = bf16[2,64,2048]{2,1,0:T(8,128)(2,1)S(1)} custom-call(s32[8,128]{1,0:T(8,128)S(1)} %broadcast_in_dim.32.refs_0_, bf16[64,2048]{1,0:T(8,128)(2,1)S(1)} %collective-permute-done.8.refs_1_, bf16[64,2048]{1,0:T(8,128)(2,1)S(1)} %collective-permute-done.9.refs_2_, bf16[1024,256]{1,0:T(8,128)(2,1)S(1)} %get-tuple-element.70.refs_3_.refs_6_.refs_2_, ...), custom_call_target="tpu_custom_call" | custom-call | flops 4140000000 | tf_op jit(solution)/shard_map/pallas_call | solution.py:467
  82.1 0.0 collective-permute-done.14.refs_1_
  82.1 0.0 collective-permute-done.15.refs_2_
  82.1 0.1 collective-permute-start.18
  82.2 2.0 %collective-permute-start.19 = (bf16[64,2048]{1,0:T(8,128)(2,1)S(1)}, bf16[64,2048]{1,0:T(8,128)(2,1)S(1)}, u32[]{:S(2)}, u32[]{:S(2)}) collective-permute-start(bf16[64,2048]{1,0:T(8,128)(2,1)S(1)} %collective-permute-done.15.refs_2_), channel_id=1, source_target_pairs={{0,2},{4,0},{8,4},{12,8},{14,12},{10,14},{6,10},{2,6},{1,3},{5,1},... | collective-permute-start | bytes 786440 | tf_op jit(solution)/shard_map/ppermute | solution.py:624
  84.2 6.9 %shard_map.89.refs_3_ = bf16[2,64,2048]{2,1,0:T(8,128)(2,1)S(1)} custom-call(s32[8,128]{1,0:T(8,128)S(1)} %broadcast_in_dim.32.refs_0_, bf16[64,2048]{1,0:T(8,128)(2,1)S(1)} %collective-permute-done.14.refs_1_, bf16[64,2048]{1,0:T(8,128)(2,1)S(1)} %collective-permute-done.15.refs_2_, bf16[1024,256]{1,0:T(8,128)(2,1)S(1)} %get-tuple-element.70.refs_3_.refs_6_.refs_2_, ...), custom_call_target="tpu_custom_call" | custom-call | flops 4140000000 | tf_op jit(solution)/shard_map/pallas_call | solution.py:467
  91.1 0.0 collective-permute-done.10.refs_4_
  91.1 0.0 collective-permute-done.11.refs_5_
  91.1 0.1 collective-permute-start.17
  91.2 2.0 %collective-permute-start.20 = (bf16[64,2048]{1,0:T(8,128)(2,1)S(1)}, bf16[64,2048]{1,0:T(8,128)(2,1)S(1)}, u32[]{:S(2)}, u32[]{:S(2)}) collective-permute-start(bf16[64,2048]{1,0:T(8,128)(2,1)S(1)} %collective-permute-done.11.refs_5_), channel_id=1, source_target_pairs={{0,2},{4,0},{8,4},{12,8},{14,12},{10,14},{6,10},{2,6},{1,3},{5,1},... | collective-permute-start | bytes 786440 | tf_op jit(solution)/shard_map/ppermute | solution.py:624
  93.2 23.9 %shard_map.92.refs_5_ = bf16[1024,2048]{1,0:T(8,128)(2,1)} custom-call(s32[8,128]{1,0:T(8,128)S(1)} %broadcast_in_dim.32.refs_0_, bf16[4,64,2048]{2,1,0:T(8,128)(2,1)S(1)} %get-tuple-element.79.refs_1_, bf16[2,64,2048]{2,1,0:T(8,128)(2,1)S(1)} %shard_map.90.refs_2_, bf16[2,64,2048]{2,1,0:T(8,128)(2,1)S(1)} %shard_map.89.refs_3_, ...), custom_call_target="tpu_custom_call", output_to_operand_aliasing={{}: (8, {})} | custom-call | flops 2875000064 | tf_op jit(solution)/shard_map/pallas_call | solution.py:512
  117.2 0.0 collective-permute-done.18.refs_1_
  117.2 0.0 collective-permute-done.19.refs_2_
  117.2 22.4 %shard_map.91.refs_1_ = bf16[2,64,2048]{2,1,0:T(8,128)(2,1)S(1)} custom-call(s32[8,128]{1,0:T(8,128)S(1)} %broadcast_in_dim.32.refs_0_, bf16[64,2048]{1,0:T(8,128)(2,1)S(1)} %collective-permute-done.18.refs_1_, bf16[64,2048]{1,0:T(8,128)(2,1)S(1)} %collective-permute-done.19.refs_2_, bf16[1024,256]{1,0:T(8,128)(2,1)S(1)} %get-tuple-element.70.refs_3_.refs_6_.refs_2_, ...), custom_call_target="tpu_custom_call" | custom-call | flops 4140000000 | tf_op jit(solution)/shard_map/pallas_call | solution.py:467
  139.6 0.0 collective-permute-done.20.refs_2_
  139.6 6.5 %shard_map.93.refs_4_ = bf16[1024,2048]{1,0:T(8,128)(2,1)} custom-call(s32[8,128]{1,0:T(8,128)S(1)} %broadcast_in_dim.32.refs_0_, bf16[2,64,2048]{2,1,0:T(8,128)(2,1)S(1)} %shard_map.91.refs_1_, bf16[64,2048]{1,0:T(8,128)(2,1)S(1)} %collective-permute-done.20.refs_2_, ...), custom_call_target="tpu_custom_call", output_to_operand_aliasing={{}: (5, {})} | custom-call | flops 2875000064 | tf_op jit(solution)/shard_map/pallas_call | solution.py:512
  146.1 0.0 collective-permute-done.17.refs_1_
  146.2 6.5 %shard_map.94 = bf16[1024,2048]{1,0:T(8,128)(2,1)} custom-call(s32[8,128]{1,0:T(8,128)S(1)} %broadcast_in_dim.32.refs_0_, bf16[64,2048]{1,0:T(8,128)(2,1)S(1)} %collective-permute-done.17.refs_1_, bf16[1024,256]{1,0:T(8,128)(2,1)S(1)} %get-tuple-element.70.refs_3_.refs_6_.refs_2_, ...), custom_call_target="tpu_custom_call", output_to_operand_aliasing={{}: (4, {})} | custom-call | flops 2875000064 | tf_op jit(solution)/shard_map/pallas_call | solution.py:512
  (7 shorter events, 0.0 us)
Async XLA Ops:
  0.6 10.9 %copy-start.3 = (bf16[256,256]{1,0:T(8,128)(2,1)S(1)}, bf16[256,256]{1,0:T(8,128)(2,1)}, u32[]{:S(2)}) copy-start(bf16[256,256]{1,0:T(8,128)(2,1)} %refs_2_.1) | copy-start | bytes 393220
  0.6 10.9 %copy-start.2 = (bf16[256,256]{1,0:T(8,128)(2,1)S(1)}, bf16[256,256]{1,0:T(8,128)(2,1)}, u32[]{:S(2)}) copy-start(bf16[256,256]{1,0:T(8,128)(2,1)} %refs_1_.1) | copy-start | bytes 393220
  0.7 3.8 %copy-start.1 = (bf16[256,2048]{1,0:T(8,128)(2,1)S(1)}, bf16[256,2048]{1,0:T(8,128)(2,1)}, u32[]{:S(2)}) copy-start(bf16[256,2048]{1,0:T(8,128)(2,1)} %q_ref.1) | copy-start | bytes 3145732
  0.7 5.9 %copy-start.4 = (s32[8,2]{0,1:T(2,128)S(1)}, s32[8,2]{0,1:T(2,128)}, u32[]{:S(2)}) copy-start(s32[8,2]{0,1:T(2,128)} %param.10) | copy-start | bytes 196
  0.7 5.9 %copy-start.5 = (s32[8,2]{0,1:T(2,128)S(1)}, s32[8,2]{0,1:T(2,128)}, u32[]{:S(2)}) copy-start(s32[8,2]{0,1:T(2,128)} %param.11) | copy-start | bytes 196
  0.7 5.9 %copy-start = (s32[8]{0:T(128)S(1)}, s32[8]{0:T(128)}, u32[]{:S(2)}) copy-start(s32[8]{0:T(128)} %length_ref.1) | copy-start | bytes 100
  2.3 5.6 %collective-permute-start.3 = (bf16[256,256]{1,0:T(8,128)(2,1)}, bf16[256,256]{1,0:T(8,128)(2,1)S(1)}, u32[]{:S(2)}, u32[]{:S(2)}) collective-permute-start(bf16[256,256]{1,0:T(8,128)(2,1)} %shard_map.85), channel_id=1, source_target_pairs={{0,2},{4,0},{8,4},{12,8},{14,12},{10,14},{6,10},{2,6},{1,3},{5,1},... | collective-permute-start | bytes 393224 | tf_op jit(solution)/shard_map/ppermute | solution.py:624
  2.8 6.6 %collective-permute-start.2 = (bf16[256,256]{1,0:T(8,128)(2,1)}, bf16[256,256]{1,0:T(8,128)(2,1)S(1)}, u32[]{:S(2)}, u32[]{:S(2)}) collective-permute-start(bf16[256,256]{1,0:T(8,128)(2,1)} %shard_map.85), channel_id=1, source_target_pairs={{0,4},{4,8},{8,12},{12,14},{14,10},{10,6},{6,2},{2,0},{1,5},{5,9},... | collective-permute-start | bytes 393224 | tf_op jit(solution)/shard_map/ppermute | solution.py:624
  4.5 21.3 %collective-permute-start = (bf16[64,2048]{1,0:T(8,128)(2,1)S(1)}, bf16[64,2048]{1,0:T(8,128)(2,1)S(1)}, u32[]{:S(2)}, u32[]{:S(2)}) collective-permute-start(bf16[64,2048]{1,0:T(8,128)(2,1)S(1)} %get-tuple-element.63), channel_id=1, source_target_pairs={{0,4},{4,8},{8,12},{12,14},{14,10},{10,6},{6,2},{2,0},{1,5},{5,9},... | collective-permute-start | bytes 786440 | tf_op jit(solution)/shard_map/ppermute | solution.py:624
  6.1 19.7 %collective-permute-start.1 = (bf16[64,2048]{1,0:T(8,128)(2,1)S(1)}, bf16[64,2048]{1,0:T(8,128)(2,1)S(1)}, u32[]{:S(2)}, u32[]{:S(2)}) collective-permute-start(bf16[64,2048]{1,0:T(8,128)(2,1)S(1)} %get-tuple-element.62), channel_id=1, source_target_pairs={{0,2},{4,0},{8,4},{12,8},{14,12},{10,14},{6,10},{2,6},{1,3},{5,1},... | collective-permute-start | bytes 786440 | tf_op jit(solution)/shard_map/ppermute | solution.py:624
  9.5 14.2 %collective-permute-start.4 = (bf16[256,256]{1,0:T(8,128)(2,1)S(1)}, bf16[256,256]{1,0:T(8,128)(2,1)S(1)}, u32[]{:S(2)}, u32[]{:S(2)}) collective-permute-start(bf16[256,256]{1,0:T(8,128)(2,1)S(1)} %collective-permute-done.2.refs_3_), channel_id=1, source_target_pairs={{0,4},{4,8},{8,12},{12,14},{14,10},{10,6},{6,2},{2,0},{1,5},{5,9},... | collective-permute-start | bytes 393224 | tf_op jit(solution)/shard_map/ppermute | solution.py:624
  11.1 12.7 %collective-permute-start.5 = (bf16[256,256]{1,0:T(8,128)(2,1)S(1)}, bf16[256,256]{1,0:T(8,128)(2,1)S(1)}, u32[]{:S(2)}, u32[]{:S(2)}) collective-permute-start(bf16[256,256]{1,0:T(8,128)(2,1)S(1)} %collective-permute-done.3.refs_4_), channel_id=1, source_target_pairs={{0,2},{4,0},{8,4},{12,8},{14,12},{10,14},{6,10},{2,6},{1,3},{5,1},... | collective-permute-start | bytes 393224 | tf_op jit(solution)/shard_map/ppermute | solution.py:624
  23.7 6.1 %collective-permute-start.6 = (bf16[256,256]{1,0:T(8,128)(2,1)S(1)}, bf16[256,256]{1,0:T(8,128)(2,1)S(1)}, u32[]{:S(2)}, u32[]{:S(2)}) collective-permute-start(bf16[256,256]{1,0:T(8,128)(2,1)S(1)} %collective-permute-done.4.refs_5_), channel_id=1, source_target_pairs={{0,4},{4,8},{8,12},{12,14},{14,10},{10,6},{6,2},{2,0},{1,5},{5,9},... | collective-permute-start | bytes 393224 | tf_op jit(solution)/shard_map/ppermute | solution.py:624
  23.8 6.6 %collective-permute-start.7 = (bf16[256,256]{1,0:T(8,128)(2,1)S(1)}, bf16[256,256]{1,0:T(8,128)(2,1)S(1)}, u32[]{:S(2)}, u32[]{:S(2)}) collective-permute-start(bf16[256,256]{1,0:T(8,128)(2,1)S(1)} %collective-permute-done.5.refs_6_), channel_id=1, source_target_pairs={{0,2},{4,0},{8,4},{12,8},{14,12},{10,14},{6,10},{2,6},{1,3},{5,1},... | collective-permute-start | bytes 393224 | tf_op jit(solution)/shard_map/ppermute | solution.py:624
  25.8 9.6 %collective-permute-start.12 = (bf16[64,2048]{1,0:T(8,128)(2,1)S(1)}, bf16[64,2048]{1,0:T(8,128)(2,1)S(1)}, u32[]{:S(2)}, u32[]{:S(2)}) collective-permute-start(bf16[64,2048]{1,0:T(8,128)(2,1)S(1)} %get-tuple-element.62), channel_id=1, source_target_pairs={{0,4},{4,8},{8,12},{12,14},{14,10},{10,6},{6,2},{2,0},{1,5},{5,9},... | collective-permute-start | bytes 786440 | tf_op jit(solution)/shard_map/ppermute | solution.py:624
  27.0 9.2 %collective-permute-start.13 = (bf16[64,2048]{1,0:T(8,128)(2,1)S(1)}, bf16[64,2048]{1,0:T(8,128)(2,1)S(1)}, u32[]{:S(2)}, u32[]{:S(2)}) collective-permute-start(bf16[64,2048]{1,0:T(8,128)(2,1)S(1)} %get-tuple-element.63), channel_id=1, source_target_pairs={{0,2},{4,0},{8,4},{12,8},{14,12},{10,14},{6,10},{2,6},{1,3},{5,1},... | collective-permute-start | bytes 786440 | tf_op jit(solution)/shard_map/ppermute | solution.py:624
  30.3 8.6 %collective-permute-start.16 = (bf16[256,256]{1,0:T(8,128)(2,1)S(1)}, bf16[256,256]{1,0:T(8,128)(2,1)S(1)}, u32[]{:S(2)}, u32[]{:S(2)}) collective-permute-start(bf16[256,256]{1,0:T(8,128)(2,1)S(1)} %collective-permute-done.6.refs_7_), channel_id=1, source_target_pairs={{0,4},{4,8},{8,12},{12,14},{14,10},{10,6},{6,2},{2,0},{1,5},{5,9},... | collective-permute-start | bytes 393224 | tf_op jit(solution)/shard_map/ppermute | solution.py:624
  33.4 40.1 %collective-permute-start.8 = (bf16[64,2048]{1,0:T(8,128)(2,1)S(1)}, bf16[64,2048]{1,0:T(8,128)(2,1)S(1)}, u32[]{:S(2)}, u32[]{:S(2)}) collective-permute-start(bf16[64,2048]{1,0:T(8,128)(2,1)S(1)} %collective-permute-done.refs_10_), channel_id=1, source_target_pairs={{0,4},{4,8},{8,12},{12,14},{14,10},{10,6},{6,2},{2,0},{1,5},{5,9},... | collective-permute-start | bytes 786440 | tf_op jit(solution)/shard_map/ppermute | solution.py:624
  33.4 40.1 %collective-permute-start.9 = (bf16[64,2048]{1,0:T(8,128)(2,1)S(1)}, bf16[64,2048]{1,0:T(8,128)(2,1)S(1)}, u32[]{:S(2)}, u32[]{:S(2)}) collective-permute-start(bf16[64,2048]{1,0:T(8,128)(2,1)S(1)} %collective-permute-done.1.refs_11_), channel_id=1, source_target_pairs={{0,2},{4,0},{8,4},{12,8},{14,12},{10,14},{6,10},{2,6},{1,3},{5,1},... | collective-permute-start | bytes 786440 | tf_op jit(solution)/shard_map/ppermute | solution.py:624
  36.2 45.9 %collective-permute-start.14 = (bf16[64,2048]{1,0:T(8,128)(2,1)S(1)}, bf16[64,2048]{1,0:T(8,128)(2,1)S(1)}, u32[]{:S(2)}, u32[]{:S(2)}) collective-permute-start(bf16[64,2048]{1,0:T(8,128)(2,1)S(1)} %collective-permute-done.12.refs_12_), channel_id=1, source_target_pairs={{0,4},{4,8},{8,12},{12,14},{14,10},{10,6},{6,2},{2,0},{1,5},{5,9},... | collective-permute-start | bytes 786440 | tf_op jit(solution)/shard_map/ppermute | solution.py:624
  39.0 43.1 %collective-permute-start.15 = (bf16[64,2048]{1,0:T(8,128)(2,1)S(1)}, bf16[64,2048]{1,0:T(8,128)(2,1)S(1)}, u32[]{:S(2)}, u32[]{:S(2)}) collective-permute-start(bf16[64,2048]{1,0:T(8,128)(2,1)S(1)} %collective-permute-done.13.refs_13_), channel_id=1, source_target_pairs={{0,2},{4,0},{8,4},{12,8},{14,12},{10,14},{6,10},{2,6},{1,3},{5,1},... | collective-permute-start | bytes 786440 | tf_op jit(solution)/shard_map/ppermute | solution.py:624
  73.5 17.6 %collective-permute-start.10 = (bf16[64,2048]{1,0:T(8,128)(2,1)S(1)}, bf16[64,2048]{1,0:T(8,128)(2,1)S(1)}, u32[]{:S(2)}, u32[]{:S(2)}) collective-permute-start(bf16[64,2048]{1,0:T(8,128)(2,1)S(1)} %collective-permute-done.8.refs_1_), channel_id=1, source_target_pairs={{0,4},{4,8},{8,12},{12,14},{14,10},{10,6},{6,2},{2,0},{1,5},{5,9},... | collective-permute-start | bytes 786440 | tf_op jit(solution)/shard_map/ppermute | solution.py:624
  73.6 17.6 %collective-permute-start.11 = (bf16[64,2048]{1,0:T(8,128)(2,1)S(1)}, bf16[64,2048]{1,0:T(8,128)(2,1)S(1)}, u32[]{:S(2)}, u32[]{:S(2)}) collective-permute-start(bf16[64,2048]{1,0:T(8,128)(2,1)S(1)} %collective-permute-done.9.refs_2_), channel_id=1, source_target_pairs={{0,2},{4,0},{8,4},{12,8},{14,12},{10,14},{6,10},{2,6},{1,3},{5,1},... | collective-permute-start | bytes 786440 | tf_op jit(solution)/shard_map/ppermute | solution.py:624
  82.1 35.0 %collective-permute-start.18 = (bf16[64,2048]{1,0:T(8,128)(2,1)S(1)}, bf16[64,2048]{1,0:T(8,128)(2,1)S(1)}, u32[]{:S(2)}, u32[]{:S(2)}) collective-permute-start(bf16[64,2048]{1,0:T(8,128)(2,1)S(1)} %collective-permute-done.14.refs_1_), channel_id=1, source_target_pairs={{0,4},{4,8},{8,12},{12,14},{14,10},{10,6},{6,2},{2,0},{1,5},{5,9},... | collective-permute-start | bytes 786440 | tf_op jit(solution)/shard_map/ppermute | solution.py:624
  82.2 35.0 %collective-permute-start.19 = (bf16[64,2048]{1,0:T(8,128)(2,1)S(1)}, bf16[64,2048]{1,0:T(8,128)(2,1)S(1)}, u32[]{:S(2)}, u32[]{:S(2)}) collective-permute-start(bf16[64,2048]{1,0:T(8,128)(2,1)S(1)} %collective-permute-done.15.refs_2_), channel_id=1, source_target_pairs={{0,2},{4,0},{8,4},{12,8},{14,12},{10,14},{6,10},{2,6},{1,3},{5,1},... | collective-permute-start | bytes 786440 | tf_op jit(solution)/shard_map/ppermute | solution.py:624
  91.1 55.0 %collective-permute-start.17 = (bf16[64,2048]{1,0:T(8,128)(2,1)S(1)}, bf16[64,2048]{1,0:T(8,128)(2,1)S(1)}, u32[]{:S(2)}, u32[]{:S(2)}) collective-permute-start(bf16[64,2048]{1,0:T(8,128)(2,1)S(1)} %collective-permute-done.10.refs_4_), channel_id=1, source_target_pairs={{0,4},{4,8},{8,12},{12,14},{14,10},{10,6},{6,2},{2,0},{1,5},{5,9},... | collective-permute-start | bytes 786440 | tf_op jit(solution)/shard_map/ppermute | solution.py:624
  91.2 48.4 %collective-permute-start.20 = (bf16[64,2048]{1,0:T(8,128)(2,1)S(1)}, bf16[64,2048]{1,0:T(8,128)(2,1)S(1)}, u32[]{:S(2)}, u32[]{:S(2)}) collective-permute-start(bf16[64,2048]{1,0:T(8,128)(2,1)S(1)} %collective-permute-done.11.refs_5_), channel_id=1, source_target_pairs={{0,2},{4,0},{8,4},{12,8},{14,12},{10,14},{6,10},{2,6},{1,3},{5,1},... | collective-permute-start | bytes 786440 | tf_op jit(solution)/shard_map/ppermute | solution.py:624
